TPU v7x, 32 devices: a whole 2x2x4 slice. The times are simulated.
32 devices in a mesh: seq: 4 (over y, x), tensor: 4 (over z), fsdp: 2 (over core).
Axes of the slice: x: 2, y: 2, z: 4, core: 2. Of those that a mesh axis runs over, the one named last changes fastest.
Arguments:
- queries: bfloat16 [2, 1024, 2048], P('fsdp', 'seq', 'tensor'), may hold values from -57 to 57
- keys: bfloat16 [2, 1024, 1024], P('fsdp', 'seq', 'tensor'), may hold values from -6 to 6
- values: bfloat16 [2, 1024, 1024], P('fsdp', 'seq', 'tensor'), may hold values from -6 to 6
- cotangent: bfloat16 [2, 1024, 5376], P('fsdp', 'seq', 'tensor'), may hold values from -96 to 96
- out_weight: bfloat16 [2048, 5376], P('tensor', 'fsdp'), may hold values from -0.078125 to 0.078125
Outputs:
- query_grads: bfloat16 [2, 1024, 2048], P('fsdp', 'seq', 'tensor')
- key_grads: bfloat16 [2, 1024, 1024], P('fsdp', 'seq', 'tensor')
- value_grads: bfloat16 [2, 1024, 1024], P('fsdp', 'seq', 'tensor')
All inputs are finite; a program needn't handle non-finite values.
Results may differ from a plain program's by a relative error of at most 0.015.
Values may be sent and summed in bfloat16 or wider, within the bound.
A program may use at most 64 MiB of HBM per device.

v0:
```python
import jax
import jax.numpy as jnp
from jax import lax
from jax.sharding import PartitionSpec as P

HEAD_SIZE = 128
WINDOW = 1024


score_scale = 168.0 ** (-0.5)
masked_score = -1e30


def passed_along(value, axis, steps):
    count = lax.axis_size(axis)
    first, last = (max(0, -steps), min(count, count - steps))
    return lax.ppermute(value, axis, [(source, source + steps) for source in range(first, last)])


def masked_scores(q_heads, k_heads, query_places, key_places):
    scores = (
        jnp.einsum("tkgd,skd->kgts", q_heads, k_heads, preferred_element_type=jnp.float32)
        * score_scale
    )
    allowed = (
        (key_places[None, :] <= query_places[:, None])
        & (key_places[None, :] > query_places[:, None] - WINDOW)
        & (key_places[None, :] >= 0)
    )
    return jnp.where(allowed, scores, masked_score)


def attention_grads(
    query_rows, grad_rows, key_rows, value_rows, query_places, key_places, key_from
):
    rows_here = query_rows.shape[0]
    key_span = key_rows.shape[0]
    kv_heads = key_rows.shape[1] // HEAD_SIZE
    head_groups = query_rows.shape[1] // (kv_heads * HEAD_SIZE)
    q_heads = query_rows.reshape(rows_here, kv_heads, head_groups, HEAD_SIZE)
    g_heads = grad_rows.reshape(rows_here, kv_heads, head_groups, HEAD_SIZE)
    k_heads = key_rows.reshape(key_span, kv_heads, HEAD_SIZE)
    v_heads = value_rows.reshape(key_span, kv_heads, HEAD_SIZE)
    scores = masked_scores(q_heads, k_heads, query_places, key_places)
    top_score = jnp.max(scores, axis=-1, keepdims=True)
    log_totals = top_score + jnp.log(jnp.sum(jnp.exp(scores - top_score), axis=-1, keepdims=True))
    probs = jnp.exp(scores - log_totals)
    probs_low = probs.astype(jnp.bfloat16)
    attended = jnp.einsum("kgts,skd->tkgd", probs_low, v_heads, preferred_element_type=jnp.float32)
    row_terms = jnp.transpose(jnp.sum(g_heads.astype(jnp.float32) * attended, axis=-1), (1, 2, 0))
    grad_probs = jnp.einsum("tkgd,skd->kgts", g_heads, v_heads, preferred_element_type=jnp.float32)
    grad_low = (probs * (grad_probs - row_terms[..., None])).astype(jnp.bfloat16)
    part_q = (
        jnp.einsum("kgts,skd->tkgd", grad_low, k_heads, preferred_element_type=jnp.float32)
        * score_scale
    )
    part_k = (
        jnp.einsum("kgts,tkgd->skd", grad_low, q_heads, preferred_element_type=jnp.float32)
        * score_scale
    )
    part_v = jnp.einsum("kgts,tkgd->skd", probs_low, g_heads, preferred_element_type=jnp.float32)
    kept_span = key_span - key_from
    return (
        part_q.reshape(rows_here, -1),
        part_k.reshape(kept_span, -1),
        part_v.reshape(kept_span, -1),
        log_totals,
        row_terms,
    )


def per_device(queries, keys, values, cotangent, out_weight):
    query_rows = queries[0]
    key_rows = keys[0]
    value_rows = values[0]
    rows_here = query_rows.shape[0]
    seq_count = lax.axis_size("seq")
    seq_place = lax.axis_index("seq")
    reach_blocks = min(WINDOW // rows_here, seq_count - 1)
    full_cotangent = lax.all_gather(cotangent[0], "tensor", axis=1, tiled=True)
    head_sums = lax.dot_general(
        full_cotangent,
        lax.all_gather(out_weight, "fsdp", axis=1, tiled=True),
        (((1,), (1,)), ((), ())),
        preferred_element_type=jnp.float32,
    )
    head_grads = head_sums.astype(jnp.bfloat16)
    earlier = [
        passed_along((key_rows, value_rows), "seq", distance)
        for distance in range(reach_blocks, 0, -1)
    ]
    window_keys = jnp.concatenate([block_pair[0] for block_pair in earlier] + [key_rows], axis=0)
    window_values = jnp.concatenate(
        [block_pair[1] for block_pair in earlier] + [value_rows], axis=0
    )
    first_place = seq_place * rows_here
    query_places = first_place + jnp.arange(rows_here, dtype=jnp.int32)
    key_places = (
        first_place
        - reach_blocks * rows_here
        + jnp.arange((reach_blocks + 1) * rows_here, dtype=jnp.int32)
    )
    own_start = reach_blocks * rows_here
    part_q, part_k, part_v, log_totals, row_terms = attention_grads(
        query_rows, head_grads, window_keys, window_values, query_places, key_places, 0
    )
    own_keys = part_k[own_start:]
    own_values = part_v[own_start:]
    for distance in range(1, reach_blocks + 1):
        offset = (reach_blocks - distance) * rows_here
        returned = passed_along(
            (part_k[offset : offset + rows_here], part_v[offset : offset + rows_here]),
            "seq",
            -distance,
        )
        own_keys = own_keys + returned[0]
        own_values = own_values + returned[1]
    return (
        part_q[None].astype(jnp.bfloat16),
        own_keys[None].astype(jnp.bfloat16),
        own_values[None].astype(jnp.bfloat16),
    )


def solution(mesh):
    return jax.shard_map(
        per_device,
        mesh=mesh,
        in_specs=(
            P("fsdp", "seq", "tensor"),
            P("fsdp", "seq", "tensor"),
            P("fsdp", "seq", "tensor"),
            P("fsdp", "seq", "tensor"),
            P("tensor", "fsdp"),
        ),
        out_specs=(
            P("fsdp", "seq", "tensor"),
            P("fsdp", "seq", "tensor"),
            P("fsdp", "seq", "tensor"),
        ),
        check_vma=False,
    )
```

profile of v0, /device:TPU:4, one launch (start us, length us, event | category | flops | bytes accessed | tf_op | source)
XLA Modules:
  0.0 143.8 jit_solution(10826845064787132863)
XLA Ops:
  7.2 0.0 all-gather.6.cloned.1.call-start
  7.2 0.7 all-gather.6.cloned.1.call-update
  7.9 0.0 all-gather.4.cloned.1.call-start
  8.0 0.7 all-gather.4.cloned.1.call-update
  8.7 1.0 copy.35
  9.7 3.4 %collective-permute-start.5 = (bf16[256,256]{0,1:T(8,128)(2,1)S(1)}, bf16[256,256]{0,1:T(8,128)(2,1)S(1)}, u32[]{:S(2)}, u32[]{:S(2)}) collective-permute-start(bf16[256,256]{0,1:T(8,128)(2,1)S(1)} %bitcast.112), channel_id=1, source_target_pairs={{0,8},{8,16},{16,24},{1,9},{9,17},{17,25},{2,10},{10,18},{18,26},{... | collective-permute-start | bytes 393224 | tf_op jit(solution)/shard_map/ppermute | solution.py:17
  13.1 1.3 collective-permute-start.4
  14.4 0.7 collective-permute-start.3
  15.1 1.0 copy.28
  16.1 1.9 %collective-permute-start.2 = (bf16[256,256]{0,1:T(8,128)(2,1)S(1)}, bf16[256,256]{0,1:T(8,128)(2,1)S(1)}, u32[]{:S(2)}, u32[]{:S(2)}) collective-permute-start(bf16[256,256]{0,1:T(8,128)(2,1)S(1)} %bitcast.108), channel_id=1, source_target_pairs={{0,8},{8,16},{16,24},{1,9},{9,17},{17,25},{2,10},{10,18},{18,26},{... | collective-permute-start | bytes 393224 | tf_op jit(solution)/shard_map/ppermute | solution.py:17
  18.0 1.3 collective-permute-start.1
  19.3 0.1 copy.33
  19.4 0.1 copy.40
  19.6 0.1 copy.74
  19.7 0.0 collective-permute-done.5
  19.8 0.7 collective-permute-start
  20.4 0.8 and_and_fusion
  21.2 0.1 copy.39
  21.4 0.0 copy-start.6
  21.4 0.1 copy.38
  21.5 0.0 copy-start.7
  21.5 0.0 collective-permute-done.3
  21.5 0.1 copy.37
  21.7 0.0 copy-start.8
  21.7 2.2 %collective-permute-done.2 = bf16[256,256]{0,1:T(8,128)(2,1)S(1)} collective-permute-done((bf16[256,256]{0,1:T(8,128)(2,1)S(1)}, bf16[256,256]{0,1:T(8,128)(2,1)S(1)}, u32[]{:S(2)}, u32[]{:S(2)}) %collective-permute-start.2) | collective-permute-done | bytes 131104 | tf_op jit(solution)/shard_map/ppermute | solution.py:17
  23.9 0.1 copy.32
  24.1 2.6 %collective-permute-done.1 = bf16[256,256]{0,1:T(8,128)(2,1)S(1)} collective-permute-done((bf16[256,256]{0,1:T(8,128)(2,1)S(1)}, bf16[256,256]{0,1:T(8,128)(2,1)S(1)}, u32[]{:S(2)}, u32[]{:S(2)}) %collective-permute-start.1) | collective-permute-done | bytes 131104 | tf_op jit(solution)/shard_map/ppermute | solution.py:17
  26.6 0.1 copy.31
  26.8 0.0 collective-permute-done
  26.8 0.1 copy.30
  26.9 0.8 fusion.5
  27.7 2.0 %copy-done = f32[2,1024,256,2]{2,1,3,0:T(8,128)} copy-done((f32[2,1024,256,2]{2,1,3,0:T(8,128)}, f32[2,1024,256,2]{2,1,3,0:T(8,128)S(1)}, u32[]{:S(2)}) %copy-start) | copy-done | bytes 4194328
  29.7 0.9 exponential_reduce_fusion
  30.7 37.1 %all-gather.6.cloned.1.call-done = bf16[1,256,5376]{1,2,0:T(8,128)(2,1)} async-done(((bf16[1,256,1344]{1,2,0:T(8,128)(2,1)}), bf16[1,256,5376]{1,2,0:T(8,128)(2,1)}) %all-gather.6.cloned.1.call-update) | async-done | bytes 2752528 | tf_op jit(solution)/shard_map/all_gather | solution.py:80
  67.8 16.2 %all-gather.4.cloned.1.call-done = bf16[512,5376]{1,0:T(8,128)(2,1)} async-done(((bf16[512,2688]{1,0:T(8,128)(2,1)}), bf16[512,5376]{1,0:T(8,128)(2,1)}) %all-gather.4.cloned.1.call-update) | async-done | bytes 5505040 | tf_op jit(solution)/shard_map/all_gather | solution.py:83
  84.0 5.0 %fusion.10 = bf16[256,512]{1,0:T(8,128)(2,1)S(1)} fusion(bf16[512,5376]{1,0:T(8,128)(2,1)} %all-gather.4.cloned.1.call-done, bf16[1,256,5376]{1,2,0:T(8,128)(2,1)} %all-gather.6.cloned.1.call-done), kind=kOutput, calls=%fused_computation.18 | convolution fusion | flops 1409417216 | bytes 8519680 | tf_op jit(solution)/shard_map/dot_general | solution.py:81
  89.0 0.1 copy.75
  89.2 3.6 %convolution_bitcast_fusion = f32[1024,2,128]{0,2,1:T(8,128)S(1)} fusion(bf16[256,2,2,128]{0,3,2,1:T(8,128)(2,1)S(1)} %bitcast.116, f32[2,1024,256,2]{2,1,3,0:T(8,128)} %copy-done, f32[2,2,256]{2,1,0:T(2,128)S(1)} %log_add_fusion, pred[256,1024]{0,1:T(8,128)(4,1)S(1)} %and_and_fusion), kind=kOutput, calls=%fused_computation.10 | convolution fusion | flops 272629760 | bytes 5771264 | tf_op jit(solution)/shard_map/kgts,tkgd->skd/dot_general | solution.py:61
  92.8 1.2 fusion.13
  94.1 2.4 %fusion.1 = bf16[2,2,256,1024]{2,3,1,0:T(8,128)(2,1)S(1)} fusion(f32[2,1024,256,2]{2,1,3,0:T(8,128)S(1)} %copy-done.1, bf16[256,2,2,128]{0,3,2,1:T(8,128)(2,1)S(1)} %bitcast.118, f32[2,2,256]{2,1,0:T(2,128)S(1)} %bitcast.126, f32[2,2,256]{2,1,0:T(2,128)S(1)} %log_add_fusion, pred[256,1024]{0,1:T(8,128)(4,1)S(1)} %and_and_fusion, ...), kind=kOutput, calls=%fused_computation.2 | convolution fusion | flops 276824064 | bytes 7348224 | tf_op jit(solution)/shard_map/tkgd,skd->kgts/dot_general | solution.py:51
  96.5 0.1 fusion.23
  96.6 0.8 copy.57
  97.4 2.9 %collective-permute-start.10 = (f32[256,256]{1,0:T(8,128)}, f32[256,256]{1,0:T(8,128)}, u32[]{:S(2)}, u32[]{:S(2)}) collective-permute-start(f32[256,256]{1,0:T(8,128)} %copy.57), channel_id=1, source_target_pairs={{16,0},{24,8},{17,1},{25,9},{18,2},{26,10},{19,3},{27,11},{20,4},{... | collective-permute-start | bytes 786440 | tf_op jit(solution)/shard_map/ppermute | solution.py:17
  100.3 0.8 fusion.7
  101.1 0.9 fusion.24
  102.0 1.8 %copy.49 = f32[256,256]{1,0:T(8,128)} copy(f32[256,256]{0,1:T(8,128)} %bitcast.107) | data formatting | bytes 524288 | tf_op jit(solution)/shard_map/slice | solution.py:112
  103.8 1.8 %copy.52 = f32[256,256]{1,0:T(8,128)} copy(f32[256,256]{0,1:T(8,128)} %bitcast.105) | data formatting | bytes 524288 | tf_op jit(solution)/shard_map/slice | solution.py:112
  105.6 0.8 copy.55
  106.4 0.1 copy.58
  106.5 0.1 copy.51
  106.7 2.0 %collective-permute-start.7 = (f32[256,256]{1,0:T(8,128)S(1)}, f32[256,256]{1,0:T(8,128)}, u32[]{:S(2)}, u32[]{:S(2)}) collective-permute-start(f32[256,256]{1,0:T(8,128)S(1)} %copy.51), channel_id=1, source_target_pairs={{16,0},{24,8},{17,1},{25,9},{18,2},{26,10},{19,3},{27,11},{20,4},{... | collective-permute-start | bytes 786440 | tf_op jit(solution)/shard_map/ppermute | solution.py:17
  108.7 1.4 collective-permute-start.11
  110.0 1.9 %collective-permute-start.9 = (f32[256,256]{1,0:T(8,128)}, f32[256,256]{1,0:T(8,128)}, u32[]{:S(2)}, u32[]{:S(2)}) collective-permute-start(f32[256,256]{1,0:T(8,128)} %copy.55), channel_id=1, source_target_pairs={{8,0},{16,8},{24,16},{9,1},{17,9},{25,17},{10,2},{18,10},{26,18},{... | collective-permute-start | bytes 786440 | tf_op jit(solution)/shard_map/ppermute | solution.py:17
  112.0 1.4 collective-permute-start.8
  113.3 0.0 collective-permute-done.10
  113.3 1.9 %collective-permute-start.6 = (f32[256,256]{1,0:T(8,128)}, f32[256,256]{1,0:T(8,128)}, u32[]{:S(2)}, u32[]{:S(2)}) collective-permute-start(f32[256,256]{1,0:T(8,128)} %copy.49), channel_id=1, source_target_pairs={{8,0},{16,8},{24,16},{9,1},{17,9},{25,17},{10,2},{18,10},{26,18},{... | collective-permute-start | bytes 786440 | tf_op jit(solution)/shard_map/ppermute | solution.py:17
  115.2 1.5 %fusion.9 = bf16[2,128,2,256]{3,1,2,0:T(8,128)(2,1)S(1)} fusion(bf16[2,2,256,1024]{2,3,1,0:T(8,128)(2,1)S(1)} %fusion.1, bf16[256,2,128]{2,0,1:T(8,128)(2,1)S(1)} %copy.33, bf16[256,2,128]{2,0,1:T(8,128)(2,1)} %copy-done.3, bf16[256,2,128]{2,0,1:T(8,128)(2,1)} %copy-done.4, bf16[256,2,128]{2,0,1:T(8,128)(2,1)} %copy-done.5), kind=kOutput, calls=%fused_computation.17 | convolution fusion | flops 270794752 | bytes 2883584 | tf_op jit(solution)/shard_map/kgts,skd->tkgd/dot_general | solution.py:54
  116.8 0.8 copy.59
  117.6 0.1 copy.56
  117.8 0.1 copy.50
  117.9 6.6 %collective-permute-done.9 = f32[256,256]{1,0:T(8,128)} collective-permute-done((f32[256,256]{1,0:T(8,128)}, f32[256,256]{1,0:T(8,128)}, u32[]{:S(2)}, u32[]{:S(2)}) %collective-permute-start.9) | collective-permute-done | bytes 262176 | tf_op jit(solution)/shard_map/ppermute | solution.py:17
  124.5 1.8 %fusion.16 = bf16[1,256,256]{2,1,0:T(8,128)(2,1)} fusion(f32[256,256]{1,0:T(8,128)} %collective-permute-done.11, f32[256,256]{1,0:T(8,128)} %collective-permute-done.10, f32[256,256]{1,0:T(8,128)S(1)} %copy.56, f32[256,256]{1,0:T(8,128)} %collective-permute-done.9), kind=kLoop, calls=%fused_computation.27 | loop fusion | flops 262144 | bytes 1179648 | tf_op jit(solution)/shard_map/convert_element_type | solution.py:121
  126.4 8.8 %collective-permute-done.6 = f32[256,256]{1,0:T(8,128)} collective-permute-done((f32[256,256]{1,0:T(8,128)}, f32[256,256]{1,0:T(8,128)}, u32[]{:S(2)}, u32[]{:S(2)}) %collective-permute-start.6) | collective-permute-done | bytes 262176 | tf_op jit(solution)/shard_map/ppermute | solution.py:17
  135.1 1.8 %fusion.15 = bf16[1,256,256]{2,1,0:T(8,128)(2,1)} fusion(f32[256,256]{1,0:T(8,128)} %collective-permute-done.8, f32[256,256]{1,0:T(8,128)} %collective-permute-done.7, f32[256,256]{1,0:T(8,128)S(1)} %copy.50, f32[256,256]{1,0:T(8,128)} %collective-permute-done.6), kind=kLoop, calls=%fused_computation.26 | loop fusion | flops 262144 | bytes 1179648 | tf_op jit(solution)/shard_map/convert_element_type | solution.py:120
  (22 shorter events, 0.1 us)
Async XLA Ops:
  7.2 12.4 %copy-start.2 = (bf16[1,256,512]{2,1,0:T(8,128)(2,1)S(1)}, bf16[1,256,512]{2,1,0:T(8,128)(2,1)}, u32[]{:S(2)}) copy-start(bf16[1,256,512]{2,1,0:T(8,128)(2,1)} %param.5) | copy-start | bytes 786436
  7.2 60.6 %all-gather.6.cloned.1.call-start = ((), (), s32[]{:S(2)}) async-start(), calls=%async_computation.1 | async-start | bytes 3440640 | tf_op jit(solution)/shard_map/all_gather | solution.py:80
  7.9 76.1 %all-gather.4.cloned.1.call-start = ((), (), s32[]{:S(2)}) async-start(), calls=%async_computation | async-start | bytes 8257536 | tf_op jit(solution)/shard_map/all_gather | solution.py:83
  9.7 10.1 %collective-permute-start.5 = (bf16[256,256]{0,1:T(8,128)(2,1)S(1)}, bf16[256,256]{0,1:T(8,128)(2,1)S(1)}, u32[]{:S(2)}, u32[]{:S(2)}) collective-permute-start(bf16[256,256]{0,1:T(8,128)(2,1)S(1)} %bitcast.112), channel_id=1, source_target_pairs={{0,8},{8,16},{16,24},{1,9},{9,17},{17,25},{2,10},{10,18},{18,26},{... | collective-permute-start | bytes 393224 | tf_op jit(solution)/shard_map/ppermute | solution.py:17
  13.1 8.3 %collective-permute-start.4 = (bf16[256,256]{0,1:T(8,128)(2,1)S(1)}, bf16[256,256]{0,1:T(8,128)(2,1)S(1)}, u32[]{:S(2)}, u32[]{:S(2)}) collective-permute-start(bf16[256,256]{0,1:T(8,128)(2,1)S(1)} %bitcast.113), channel_id=1, source_target_pairs={{0,16},{8,24},{1,17},{9,25},{2,18},{10,26},{3,19},{11,27},{4,20},{... | collective-permute-start | bytes 393224 | tf_op jit(solution)/shard_map/ppermute | solution.py:17
  14.4 7.2 %collective-permute-start.3 = (bf16[256,256]{0,1:T(8,128)(2,1)S(1)}, bf16[256,256]{0,1:T(8,128)(2,1)S(1)}, u32[]{:S(2)}, u32[]{:S(2)}) collective-permute-start(bf16[256,256]{0,1:T(8,128)(2,1)S(1)} %bitcast.114), channel_id=1, source_target_pairs={{0,24},{1,25},{2,26},{3,27},{4,28},{5,29},{6,30},{7,31}} | collective-permute-start | bytes 393224 | tf_op jit(solution)/shard_map/ppermute | solution.py:17
  16.1 7.9 %collective-permute-start.2 = (bf16[256,256]{0,1:T(8,128)(2,1)S(1)}, bf16[256,256]{0,1:T(8,128)(2,1)S(1)}, u32[]{:S(2)}, u32[]{:S(2)}) collective-permute-start(bf16[256,256]{0,1:T(8,128)(2,1)S(1)} %bitcast.108), channel_id=1, source_target_pairs={{0,8},{8,16},{16,24},{1,9},{9,17},{17,25},{2,10},{10,18},{18,26},{... | collective-permute-start | bytes 393224 | tf_op jit(solution)/shard_map/ppermute | solution.py:17
  18.0 8.6 %collective-permute-start.1 = (bf16[256,256]{0,1:T(8,128)(2,1)S(1)}, bf16[256,256]{0,1:T(8,128)(2,1)S(1)}, u32[]{:S(2)}, u32[]{:S(2)}) collective-permute-start(bf16[256,256]{0,1:T(8,128)(2,1)S(1)} %bitcast.109), channel_id=1, source_target_pairs={{0,16},{8,24},{1,17},{9,25},{2,18},{10,26},{3,19},{11,27},{4,20},{... | collective-permute-start | bytes 393224 | tf_op jit(solution)/shard_map/ppermute | solution.py:17
  19.8 7.0 %collective-permute-start = (bf16[256,256]{0,1:T(8,128)(2,1)S(1)}, bf16[256,256]{0,1:T(8,128)(2,1)S(1)}, u32[]{:S(2)}, u32[]{:S(2)}) collective-permute-start(bf16[256,256]{0,1:T(8,128)(2,1)S(1)} %bitcast.111), channel_id=1, source_target_pairs={{0,24},{1,25},{2,26},{3,27},{4,28},{5,29},{6,30},{7,31}} | collective-permute-start | bytes 393224 | tf_op jit(solution)/shard_map/ppermute | solution.py:17
  21.4 71.4 %copy-start.6 = (bf16[256,2,128]{2,0,1:T(8,128)(2,1)}, bf16[256,2,128]{2,0,1:T(8,128)(2,1)S(1)}, u32[]{:S(2)}) copy-start(bf16[256,2,128]{2,0,1:T(8,128)(2,1)S(1)} %copy.39) | copy-start | bytes 393220
  21.5 71.3 %copy-start.7 = (bf16[256,2,128]{2,0,1:T(8,128)(2,1)}, bf16[256,2,128]{2,0,1:T(8,128)(2,1)S(1)}, u32[]{:S(2)}) copy-start(bf16[256,2,128]{2,0,1:T(8,128)(2,1)S(1)} %copy.38) | copy-start | bytes 393220
  21.7 71.1 %copy-start.8 = (bf16[256,2,128]{2,0,1:T(8,128)(2,1)}, bf16[256,2,128]{2,0,1:T(8,128)(2,1)S(1)}, u32[]{:S(2)}) copy-start(bf16[256,2,128]{2,0,1:T(8,128)(2,1)S(1)} %copy.37) | copy-start | bytes 393220
  24.0 6.6 %copy-start.3 = (bf16[256,2,128]{2,0,1:T(8,128)(2,1)}, bf16[256,2,128]{2,0,1:T(8,128)(2,1)S(1)}, u32[]{:S(2)}) copy-start(bf16[256,2,128]{2,0,1:T(8,128)(2,1)S(1)} %copy.32) | copy-start | bytes 393220
  26.7 3.9 %copy-start.4 = (bf16[256,2,128]{2,0,1:T(8,128)(2,1)}, bf16[256,2,128]{2,0,1:T(8,128)(2,1)S(1)}, u32[]{:S(2)}) copy-start(bf16[256,2,128]{2,0,1:T(8,128)(2,1)S(1)} %copy.31) | copy-start | bytes 393220
  26.9 3.8 %copy-start.5 = (bf16[256,2,128]{2,0,1:T(8,128)(2,1)}, bf16[256,2,128]{2,0,1:T(8,128)(2,1)S(1)}, u32[]{:S(2)}) copy-start(bf16[256,2,128]{2,0,1:T(8,128)(2,1)S(1)} %copy.30) | copy-start | bytes 393220
  27.7 2.0 %copy-start = (f32[2,1024,256,2]{2,1,3,0:T(8,128)}, f32[2,1024,256,2]{2,1,3,0:T(8,128)S(1)}, u32[]{:S(2)}) copy-start(f32[2,1024,256,2]{2,1,3,0:T(8,128)S(1)} %get-tuple-element.18) | copy-start | bytes 12582916
  89.1 3.7 %copy-start.1 = (f32[2,1024,256,2]{2,1,3,0:T(8,128)S(1)}, f32[2,1024,256,2]{2,1,3,0:T(8,128)}, u32[]{:S(2)}) copy-start(f32[2,1024,256,2]{2,1,3,0:T(8,128)} %copy-done) | copy-start | bytes 12582916
  97.4 15.9 %collective-permute-start.10 = (f32[256,256]{1,0:T(8,128)}, f32[256,256]{1,0:T(8,128)}, u32[]{:S(2)}, u32[]{:S(2)}) collective-permute-start(f32[256,256]{1,0:T(8,128)} %copy.57), channel_id=1, source_target_pairs={{16,0},{24,8},{17,1},{25,9},{18,2},{26,10},{19,3},{27,11},{20,4},{... | collective-permute-start | bytes 786440 | tf_op jit(solution)/shard_map/ppermute | solution.py:17
  106.7 19.7 %collective-permute-start.7 = (f32[256,256]{1,0:T(8,128)S(1)}, f32[256,256]{1,0:T(8,128)}, u32[]{:S(2)}, u32[]{:S(2)}) collective-permute-start(f32[256,256]{1,0:T(8,128)S(1)} %copy.51), channel_id=1, source_target_pairs={{16,0},{24,8},{17,1},{25,9},{18,2},{26,10},{19,3},{27,11},{20,4},{... | collective-permute-start | bytes 786440 | tf_op jit(solution)/shard_map/ppermute | solution.py:17
  108.7 9.2 %collective-permute-start.11 = (f32[256,256]{1,0:T(8,128)S(1)}, f32[256,256]{1,0:T(8,128)}, u32[]{:S(2)}, u32[]{:S(2)}) collective-permute-start(f32[256,256]{1,0:T(8,128)S(1)} %copy.58), channel_id=1, source_target_pairs={{24,0},{25,1},{26,2},{27,3},{28,4},{29,5},{30,6},{31,7}} | collective-permute-start | bytes 786440 | tf_op jit(solution)/shard_map/ppermute | solution.py:17
  110.0 14.5 %collective-permute-start.9 = (f32[256,256]{1,0:T(8,128)}, f32[256,256]{1,0:T(8,128)}, u32[]{:S(2)}, u32[]{:S(2)}) collective-permute-start(f32[256,256]{1,0:T(8,128)} %copy.55), channel_id=1, source_target_pairs={{8,0},{16,8},{24,16},{9,1},{17,9},{25,17},{10,2},{18,10},{26,18},{... | collective-permute-start | bytes 786440 | tf_op jit(solution)/shard_map/ppermute | solution.py:17
  112.0 14.4 %collective-permute-start.8 = (f32[256,256]{1,0:T(8,128)}, f32[256,256]{1,0:T(8,128)}, u32[]{:S(2)}, u32[]{:S(2)}) collective-permute-start(f32[256,256]{1,0:T(8,128)} %copy.52), channel_id=1, source_target_pairs={{24,0},{25,1},{26,2},{27,3},{28,4},{29,5},{30,6},{31,7}} | collective-permute-start | bytes 786440 | tf_op jit(solution)/shard_map/ppermute | solution.py:17
  113.3 21.8 %collective-permute-start.6 = (f32[256,256]{1,0:T(8,128)}, f32[256,256]{1,0:T(8,128)}, u32[]{:S(2)}, u32[]{:S(2)}) collective-permute-start(f32[256,256]{1,0:T(8,128)} %copy.49), channel_id=1, source_target_pairs={{8,0},{16,8},{24,16},{9,1},{17,9},{25,17},{10,2},{18,10},{26,18},{... | collective-permute-start | bytes 786440 | tf_op jit(solution)/shard_map/ppermute | solution.py:17
Sparse Core Ops, SparseCore 0:
  9.6 58.1 all-gather.5
  69.3 14.5 all-gather.3
where the time goes:
time: 144 us
  waiting for transfers between devices  74.9 us (52%)
  starting transfers between devices  20.8 us (14%)
  matrix products  15.4 us (11%)
  between operations  14.5 us (10%)
  local copies, waits for them, and re-layouts  12.8 us (9%)
  other arithmetic  5.4 us (4%)
    all_gather x1, waiting for transfers between devices, per_device(): full_cotangent = lax.all_gather(cotangent[0], 'tensor', axis=1, tiled=True)  37.1 us
    ppermute x12, starting transfers between devices, passed_along(): lax.ppermute(value, axis, [(source, source + steps) for source in range(f...  20.7 us
    ppermute x12, waiting for transfers between devices, passed_along(): lax.ppermute(value, axis, [(source, source + steps) for source in range(f...  20.2 us
    all_gather x1, waiting for transfers between devices, per_device(): lax.all_gather(out_weight, 'fsdp', axis=1, tiled=True)  16.2 us
    dot_general x1, matrix products, per_device(): lax.dot_general(full_cotangent, lax.all_gather(out_weight, 'fsdp', axis=1...  5.04 us
    unnamed x21, local copies, waits for them, and re-layouts  4.91 us
    slice x4, local copies, waits for them, and re-layouts, per_device(): part_k[offset:offset + rows_here]  4.59 us
    dot_general x1, matrix products, attention_grads(): jnp.einsum('kgts,tkgd->skd', probs_low, g_heads, preferred_element_type=j...  3.62 us
  transfers between devices with their start and end apart: 14, of which 6 were waited for; matrix products, arithmetic and copies ran while one was open for 11% of the time, Pallas kernels for 0%

commit v1 on v0

v1 whole, which is shorter than its diff:
```python
import functools

import jax
import jax.numpy as jnp
from jax import lax
from jax.experimental import pallas as pl
from jax.experimental.pallas import tpu as pltpu
from jax.sharding import PartitionSpec as P

HEAD_SIZE = 128
WINDOW = 1024
CHUNK = 128

score_scale = 168.0 ** (-0.5)
masked_score = -1e30
MESH = pl.DeviceIdType.MESH
NT = (((1,), (1,)), ((), ()))


def dot(a, b):
    return jnp.dot(a, b, preferred_element_type=jnp.float32)


def dot_nt(a, b):
    return lax.dot_general(a, b, NT, preferred_element_type=jnp.float32)


def kernel(
    n_seq, n_tensor, n_fsdp, reach,
    q_ref, k_ref, v_ref, c_ref, w_ref,
    dq_ref, dk_ref, dv_ref,
    c_all, w_all, w_cut, k_in, v_in, q_in, lse_own, lse_in, row_own, row_in, g_own, g_in,
    s_buf, p_own, p_late, att, k_turn, v_turn, top, total, turned, dq_acc, dk_acc, dv_acc,
    c_loc, w_loc, w_send, w_recv, right_send, right_recv, left_send, left_recv,
    kv_send, kv_recv, lse_send, lse_recv, g_send, g_recv,
):
    rows = q_ref.shape[0]
    kv_heads = k_ref.shape[1] // HEAD_SIZE
    groups = q_ref.shape[1] // k_ref.shape[1]
    chunks = rows // CHUNK
    features = c_ref.shape[1]
    fsdp_features = w_ref.shape[1]
    me_s, me_t, me_f = lax.axis_index("seq"), lax.axis_index("tensor"), lax.axis_index("fsdp")

    def seq_at(offset):
        return {"seq": lax.rem(me_s + offset + n_seq, n_seq)}

    def tensor_at(offset):
        return {"tensor": lax.rem(me_t + offset + n_tensor, n_tensor)}

    def fsdp_at(offset):
        return {"fsdp": lax.rem(me_f + offset + n_fsdp, n_fsdp)}

    seq_offsets = sorted({d % n_seq for r in range(1, reach + 1) for d in (r, -r)} - {0})
    tensor_offsets = sorted({1 % n_tensor, (n_tensor - 1) % n_tensor} - {0})
    peers = (
        [seq_at(d) for d in seq_offsets]
        + [tensor_at(d) for d in tensor_offsets]
        + [fsdp_at(d) for d in range(1, n_fsdp)]
    )
    barrier = pltpu.get_barrier_semaphore()
    for peer in peers:
        pl.semaphore_signal(barrier, inc=1, device_id=peer, device_id_type=MESH)
    pl.semaphore_wait(barrier, len(peers))

    def remote(src, dst, send, recv, peer):
        return pltpu.make_async_remote_copy(
            src_ref=src, dst_ref=dst, send_sem=send, recv_sem=recv,
            device_id=peer, device_id_type=MESH,
        )

    def has_earlier(d):
        return me_s >= d

    def has_later(d):
        return me_s + d < n_seq

    def right_copy(c, s):
        place = pl.ds(c * CHUNK, CHUNK)
        slot = lax.rem(me_t - s + n_tensor, n_tensor)
        src = c_ref.at[place] if s == 0 else c_all.at[slot, place]
        return remote(src, c_all.at[slot, place], right_send.at[c, s], right_recv.at[c, s], tensor_at(1))

    def left_copy(c, s):
        place = pl.ds(c * CHUNK, CHUNK)
        slot = lax.rem(me_t + s, n_tensor)
        src = c_ref.at[place] if s == 0 else c_all.at[slot, place]
        return remote(src, c_all.at[slot, place], left_send.at[c, s], left_recv.at[c, s], tensor_at(-1))

    def right_sends(s):
        return (me_t + 1 < n_tensor) & (me_t >= s)

    def left_sends(s):
        return (me_t >= 1) & (me_t + s < n_tensor)

    def w_copy(o):
        return remote(w_ref, w_all.at[me_f], w_send.at[o], w_recv.at[o], fsdp_at(o))

    def key_copies(d):
        return [
            remote(k_ref, k_in.at[d - 1], kv_send.at[0, d], kv_recv.at[0, d], seq_at(d)),
            remote(v_ref, v_in.at[d - 1], kv_send.at[1, d], kv_recv.at[1, d], seq_at(d)),
        ]

    def query_copy(d):
        return remote(q_ref, q_in.at[d - 1], kv_send.at[2, d], kv_recv.at[2, d], seq_at(-d))

    def lse_copy(d):
        return remote(lse_own, lse_in.at[d - 1], lse_send.at[d], lse_recv.at[d], seq_at(-d))

    def grad_copies(c, d):
        place = pl.ds(c * CHUNK, CHUNK)
        return [
            remote(g_own.at[place], g_in.at[d - 1, place], g_send.at[0, c, d], g_recv.at[0, c, d], seq_at(-d)),
            remote(row_own.at[c], row_in.at[c, d - 1], g_send.at[1, c, d], g_recv.at[1, c, d], seq_at(-d)),
        ]

    for c in range(chunks):
        @pl.when(right_sends(0))
        def _():
            right_copy(c, 0).start()

        @pl.when(left_sends(0))
        def _():
            left_copy(c, 0).start()
    for o in range(1, n_fsdp):
        w_copy(o).start()
    for d in range(1, reach + 1):
        @pl.when(has_later(d))
        def _():
            for copy in key_copies(d):
                copy.start()

        @pl.when(has_earlier(d))
        def _():
            query_copy(d).start()
    own_c = pltpu.make_async_copy(c_ref, c_all.at[me_t], c_loc)
    own_c.start()
    own_w = pltpu.make_async_copy(w_ref, w_all.at[me_f], w_loc)
    own_w.start()

    def lanes(h):
        return pl.ds(pl.multiple_of(h * HEAD_SIZE, HEAD_SIZE), HEAD_SIZE)

    def key_block(d):
        return k_ref if d == 0 else k_in.at[d - 1]

    def value_block(d):
        return v_ref if d == 0 else v_in.at[d - 1]

    def on_earlier(d, do):
        if d == 0:
            do()
        else:
            pl.when(has_earlier(d))(do)

    def masked(scores, d):
        shape = (rows, rows)
        if d == 0:
            j, i = lax.broadcasted_iota(jnp.int32, shape, 0), lax.broadcasted_iota(jnp.int32, shape, 1)
            return jnp.where(j <= i, scores, masked_score)
        if (d + 1) * rows - 1 >= WINDOW:
            j, i = lax.broadcasted_iota(jnp.int32, shape, 0), lax.broadcasted_iota(jnp.int32, shape, 1)
            return jnp.where(j - i > d * rows - WINDOW, scores, masked_score)
        return scores

    lse_own[...] = jnp.zeros_like(lse_own)
    row_own[...] = jnp.zeros_like(row_own)
    for d in range(1, reach + 1):
        @pl.when(has_earlier(d))
        def _():
            for copy in key_copies(d):
                copy.wait_recv()

    @pl.loop(0, kv_heads)
    def _(kv):
        for d in range(reach + 1):
            def turn():
                k_turn[kv, d] = key_block(d)[:, lanes(kv)].T
                v_turn[kv, d] = value_block(d)[:, lanes(kv)].T
            on_earlier(d, turn)
        for group in range(groups):
            h = kv * groups + group
            q = q_ref[:, lanes(h)]
            for d in range(reach + 1):
                def score():
                    scores = masked(dot_nt(key_block(d)[:, lanes(kv)], q) * score_scale, d)
                    s_buf[d] = scores
                    high = jnp.max(scores, axis=0, keepdims=True)
                    top[...] = high if d == 0 else jnp.maximum(top[...], high)
                on_earlier(d, score)
            for d in range(reach + 1):
                def add():
                    part = jnp.sum(jnp.exp(s_buf[d] - top[...]), axis=0, keepdims=True)
                    total[...] = part if d == 0 else total[...] + part
                on_earlier(d, add)
            lse = top[...] + jnp.log(total[...])
            lse_own[pl.ds(h, 1), :] = lse
            for d in range(reach + 1):
                def spread():
                    low = jnp.exp(s_buf[d] - lse_own[pl.ds(h, 1), :]).astype(jnp.bfloat16)
                    p_own[h, d] = low
                    part = dot(v_turn[kv, d], low)
                    turned[...] = part if d == 0 else turned[...] + part
                on_earlier(d, spread)
            att[h] = turned[...].T

    for d in range(1, reach + 1):
        @pl.when(has_earlier(d))
        def _():
            lse_copy(d).start()

    own_w.wait()
    for o in range(1, n_fsdp):
        w_copy(o).wait_recv()
    per_shard = fsdp_features // features
    for t in range(n_tensor):
        start = (t % per_shard) * features
        w_cut[t] = w_all[t // per_shard, :, start : start + features]

    for d in range(1, reach + 1):
        @pl.when(has_later(d))
        def _():
            query_copy(d).wait_recv()
            lse_copy(d).wait_recv()

            @pl.loop(0, kv_heads)
            def _(kv):
                for group in range(groups):
                    h = kv * groups + group
                    scores = masked(dot_nt(k_ref[:, lanes(kv)], q_in[d - 1, :, lanes(h)]) * score_scale, d)
                    p_late[h, d - 1] = jnp.exp(scores - lse_in[d - 1, pl.ds(h, 1), :]).astype(jnp.bfloat16)

    dk_acc[...] = jnp.zeros_like(dk_acc)
    dv_acc[...] = jnp.zeros_like(dv_acc)
    own_c.wait()

    def late_keys(c):
        place = pl.ds(c * CHUNK, CHUNK)
        for d in range(1, reach + 1):
            @pl.when(has_later(d))
            def _():
                for copy in grad_copies(c, d):
                    copy.wait_recv()

                @pl.loop(0, kv_heads)
                def _(kv):
                    for group in range(groups):
                        h = kv * groups + group
                        g = g_in[d - 1, place, lanes(h)]
                        probs = p_late[h, d - 1, :, place]
                        slope = dot_nt(v_ref[:, lanes(kv)], g) - row_in[c, d - 1, pl.ds(h, 1), :]
                        low = (probs.astype(jnp.float32) * slope).astype(jnp.bfloat16)
                        dk_acc[kv] += dot(low, q_in[d - 1, place, lanes(h)])
                        dv_acc[kv] += dot(probs, g)

    for c in range(chunks):
        place = pl.ds(c * CHUNK, CHUNK)
        sums = dot_nt(c_all[me_t, place], w_cut[me_t])
        for s in range(1, n_tensor):
            @pl.when(me_t >= s)
            def _():
                right_copy(c, s - 1).wait_recv()

            if s < n_tensor - 1:
                @pl.when(right_sends(s))
                def _():
                    right_copy(c, s).start()

            @pl.when(me_t + s < n_tensor)
            def _():
                left_copy(c, s - 1).wait_recv()

            if s < n_tensor - 1:
                @pl.when(left_sends(s))
                def _():
                    left_copy(c, s).start()
        for s in range(1, n_tensor):
            slot = lax.rem(me_t + s, n_tensor)
            sums += dot_nt(c_all[slot, place], w_cut[slot])
        g_own[place] = sums.astype(jnp.bfloat16)

        @pl.loop(0, kv_heads * groups)
        def _(h):
            product = g_own[place, lanes(h)].astype(jnp.float32) * att[h, place]
            row = lax.dot_general(
                jnp.ones((8, HEAD_SIZE), jnp.float32), product, NT,
                precision=lax.Precision.HIGHEST, preferred_element_type=jnp.float32,
            )
            row_own[c, pl.ds(h, 1), :] = row[0:1]

        for d in range(1, reach + 1):
            @pl.when(has_earlier(d))
            def _():
                for copy in grad_copies(c, d):
                    copy.start()

        @pl.loop(0, kv_heads)
        def _(kv):
            for group in range(groups):
                h = kv * groups + group
                g = g_own[place, lanes(h)]
                row = row_own[c, pl.ds(h, 1), :]
                for d in range(reach + 1):
                    def query_part():
                        probs = p_own[h, d, :, place]
                        slope = dot_nt(value_block(d)[:, lanes(kv)], g) - row
                        low = (probs.astype(jnp.float32) * slope).astype(jnp.bfloat16)
                        part = dot(k_turn[kv, d], low)
                        if d == 0:
                            dq_acc[...] = part
                            dk_acc[kv] += dot(low, q_ref[place, lanes(h)])
                            dv_acc[kv] += dot(probs, g)
                        else:
                            dq_acc[...] += part
                    on_earlier(d, query_part)
                dq_ref[place, lanes(h)] = (dq_acc[...] * score_scale).T.astype(jnp.bfloat16)

        if c > 0:
            late_keys(c - 1)
    late_keys(chunks - 1)
    for kv in range(kv_heads):
        lane = slice(kv * HEAD_SIZE, (kv + 1) * HEAD_SIZE)
        dk_ref[:, lane] = (dk_acc[kv] * score_scale).astype(jnp.bfloat16)
        dv_ref[:, lane] = dv_acc[kv].astype(jnp.bfloat16)

    for o in range(1, n_fsdp):
        w_copy(o).wait_send()
    for c in range(chunks):
        for s in range(n_tensor - 1):
            @pl.when(right_sends(s))
            def _():
                right_copy(c, s).wait_send()

            @pl.when(left_sends(s))
            def _():
                left_copy(c, s).wait_send()
    for d in range(1, reach + 1):
        @pl.when(has_later(d))
        def _():
            for copy in key_copies(d):
                copy.wait_send()

        @pl.when(has_earlier(d))
        def _():
            query_copy(d).wait_send()
            lse_copy(d).wait_send()
            for c in range(chunks):
                for copy in grad_copies(c, d):
                    copy.wait_send()


def per_device(mesh, queries, keys, values, cotangent, out_weight):
    n_seq, n_tensor, n_fsdp = mesh.shape["seq"], mesh.shape["tensor"], mesh.shape["fsdp"]
    q, k, v, c = queries[0], keys[0], values[0], cotangent[0]
    rows = q.shape[0]
    reach = min(WINDOW // rows, n_seq - 1)
    heads, kv_heads = q.shape[1] // HEAD_SIZE, k.shape[1] // HEAD_SIZE
    chunks = rows // CHUNK
    bf16, f32 = jnp.bfloat16, jnp.float32
    vmem = pl.BlockSpec(memory_space=pltpu.VMEM)
    hbm = pl.BlockSpec(memory_space=pl.ANY)
    dma = pltpu.SemaphoreType.DMA
    dq, dk, dv = pl.pallas_call(
        functools.partial(kernel, n_seq, n_tensor, n_fsdp, reach),
        out_shape=[jax.ShapeDtypeStruct(x.shape, bf16) for x in (q, k, v)],
        in_specs=[vmem, vmem, vmem, hbm, hbm],
        out_specs=[vmem] * 3,
        scratch_shapes=[
            pltpu.VMEM((n_tensor,) + c.shape, bf16),
            pltpu.VMEM((n_fsdp,) + out_weight.shape, bf16),
            pltpu.VMEM((n_tensor, out_weight.shape[0], c.shape[1]), bf16),
            pltpu.VMEM((reach,) + k.shape, bf16),
            pltpu.VMEM((reach,) + v.shape, bf16),
            pltpu.VMEM((reach,) + q.shape, bf16),
            pltpu.VMEM((8, rows), f32),
            pltpu.VMEM((reach, 8, rows), f32),
            pltpu.VMEM((chunks, 8, CHUNK), f32),
            pltpu.VMEM((chunks, reach, 8, CHUNK), f32),
            pltpu.VMEM(q.shape, bf16),
            pltpu.VMEM((reach,) + q.shape, bf16),
            pltpu.VMEM((reach + 1, rows, rows), f32),
            pltpu.VMEM((heads, reach + 1, rows, rows), bf16),
            pltpu.VMEM((heads, reach, rows, rows), bf16),
            pltpu.VMEM((heads, rows, HEAD_SIZE), f32),
            pltpu.VMEM((kv_heads, reach + 1, HEAD_SIZE, rows), bf16),
            pltpu.VMEM((kv_heads, reach + 1, HEAD_SIZE, rows), bf16),
            pltpu.VMEM((1, rows), f32),
            pltpu.VMEM((1, rows), f32),
            pltpu.VMEM((HEAD_SIZE, rows), f32),
            pltpu.VMEM((HEAD_SIZE, CHUNK), f32),
            pltpu.VMEM((kv_heads, rows, HEAD_SIZE), f32),
            pltpu.VMEM((kv_heads, rows, HEAD_SIZE), f32),
            dma, dma,
            dma((n_fsdp,)), dma((n_fsdp,)),
            dma((chunks, n_tensor)), dma((chunks, n_tensor)),
            dma((chunks, n_tensor)), dma((chunks, n_tensor)),
            dma((3, reach + 1)), dma((3, reach + 1)),
            dma((reach + 1,)), dma((reach + 1,)),
            dma((2, chunks, reach + 1)), dma((2, chunks, reach + 1)),
        ],
        compiler_params=pltpu.CompilerParams(
            collective_id=0, has_side_effects=True, vmem_limit_bytes=56 * 2**20
        ),
        cost_estimate=pl.CostEstimate(flops=4 * 10**9, bytes_accessed=8 * 10**6, transcendentals=4 * 10**6),
    )(q, k, v, c, out_weight)
    return dq[None], dk[None], dv[None]


def solution(mesh):
    parts = P("fsdp", "seq", "tensor")
    return jax.shard_map(
        functools.partial(per_device, mesh),
        mesh=mesh,
        in_specs=(parts, parts, parts, parts, P("tensor", "fsdp")),
        out_specs=(parts, parts, parts),
        check_vma=False,
    )
```

time: 144 us -> 80.3 us (0.56)
  the two profiles are of different devices: /device:TPU:4 before, /device:TPU:0 now
where the time goes in v1:
time: 80.3 us; the launch traced here: 80 us
  Pallas kernels  72.3 us (90%)
  local copies, waits for them, and re-layouts  7.04 us (9%)
    pallas_call x1, Pallas kernels, per_device(): pl.pallas_call(functools.partial(kernel, n_seq, n_tensor, n_fsdp, reach),...  72.3 us
    unnamed x4, local copies, waits for them, and re-layouts  7.04 us

profile of v1, /device:TPU:0, one launch (start us, length us, event | category | flops | bytes accessed | tf_op | source)
XLA Modules:
  0.0 80.0 jit_solution(13695126066345732828)
XLA Ops:
  0.6 2.2 %copy.8 = bf16[1,256,1344]{2,1,0:T(8,128)(2,1)} copy(bf16[1,256,1344]{1,2,0:T(8,128)(2,1)} %param.8) | data formatting | bytes 1376256 | tf_op args[3]
  2.9 72.3 %shard_map.76 = (bf16[256,512]{1,0:T(8,128)(2,1)}, bf16[256,256]{1,0:T(8,128)(2,1)}, bf16[256,256]{1,0:T(8,128)(2,1)}) custom-call(bf16[256,512]{1,0:T(8,128)(2,1)} %bitcast.11, bf16[256,256]{1,0:T(8,128)(2,1)} %bitcast.12, bf16[256,256]{1,0:T(8,128)(2,1)} %bitcast.13, bf16[256,1344]{1,0:T(8,128)(2,1)} %bitcast.7, bf16[512,2688]{1,0:T(8,128)(2,1)} %w_ref.1), custom_call_target="tpu_custom_call" | custom-call | flops 4000000000 | bytes 8000000 | tf_op jit(solution)/shard_map/pallas_call | solution.py:364
  75.2 1.7 %copy.12 = bf16[1,256,512]{2,1,0:T(8,128)(2,1)} copy(bf16[1,256,512]{2,1,0:T(8,128)(2,1)} %bitcast.8) | data formatting | bytes 524288
  76.9 1.6 %copy.13 = bf16[1,256,256]{2,1,0:T(8,128)(2,1)} copy(bf16[1,256,256]{2,1,0:T(8,128)(2,1)} %bitcast.10) | data formatting | bytes 262144
  78.5 1.6 %copy.14 = bf16[1,256,256]{2,1,0:T(8,128)(2,1)} copy(bf16[1,256,256]{2,1,0:T(8,128)(2,1)} %bitcast.9) | data formatting | bytes 262144

commit v2 on v1

--- a/solution.py
+++ b/solution.py
@@ -29,7 +29,7 @@
     n_seq, n_tensor, n_fsdp, reach,
     q_ref, k_ref, v_ref, c_ref, w_ref,
     dq_ref, dk_ref, dv_ref,
-    c_all, w_all, w_cut, k_in, v_in, q_in, lse_own, lse_in, row_own, row_in, g_own, g_in,
+    c_all, w_all, k_in, v_in, q_in, lse_own, lse_in, row_own, row_in, g_own, g_in,
     s_buf, p_own, p_late, att, k_turn, v_turn, top, total, turned, dq_acc, dk_acc, dv_acc,
     c_loc, w_loc, w_send, w_recv, right_send, right_recv, left_send, left_recv,
     kv_send, kv_recv, lse_send, lse_recv, g_send, g_recv,
@@ -38,7 +38,7 @@
     kv_heads = k_ref.shape[1] // HEAD_SIZE
     groups = q_ref.shape[1] // k_ref.shape[1]
     chunks = rows // CHUNK
-    features = c_ref.shape[1]
+    features = c_ref.shape[0]
     fsdp_features = w_ref.shape[1]
     me_s, me_t, me_f = lax.axis_index("seq"), lax.axis_index("tensor"), lax.axis_index("fsdp")
 
@@ -75,17 +75,22 @@
     def has_later(d):
         return me_s + d < n_seq
 
+    def block(slot):
+        return pl.ds(pl.multiple_of(slot * features, 16), features)
+
     def right_copy(c, s):
         place = pl.ds(c * CHUNK, CHUNK)
         slot = lax.rem(me_t - s + n_tensor, n_tensor)
-        src = c_ref.at[place] if s == 0 else c_all.at[slot, place]
-        return remote(src, c_all.at[slot, place], right_send.at[c, s], right_recv.at[c, s], tensor_at(1))
+        there = c_all.at[block(slot), place]
+        src = c_ref.at[:, place] if s == 0 else there
+        return remote(src, there, right_send.at[c, s], right_recv.at[c, s], tensor_at(1))
 
     def left_copy(c, s):
         place = pl.ds(c * CHUNK, CHUNK)
         slot = lax.rem(me_t + s, n_tensor)
-        src = c_ref.at[place] if s == 0 else c_all.at[slot, place]
-        return remote(src, c_all.at[slot, place], left_send.at[c, s], left_recv.at[c, s], tensor_at(-1))
+        there = c_all.at[block(slot), place]
+        src = c_ref.at[:, place] if s == 0 else there
+        return remote(src, there, left_send.at[c, s], left_recv.at[c, s], tensor_at(-1))
 
     def right_sends(s):
         return (me_t + 1 < n_tensor) & (me_t >= s)
@@ -111,7 +116,7 @@
     def grad_copies(c, d):
         place = pl.ds(c * CHUNK, CHUNK)
         return [
-            remote(g_own.at[place], g_in.at[d - 1, place], g_send.at[0, c, d], g_recv.at[0, c, d], seq_at(-d)),
+            remote(g_own.at[:, place], g_in.at[d - 1, :, place], g_send.at[0, c, d], g_recv.at[0, c, d], seq_at(-d)),
             remote(row_own.at[c], row_in.at[c, d - 1], g_send.at[1, c, d], g_recv.at[1, c, d], seq_at(-d)),
         ]
 
@@ -134,7 +139,36 @@
         @pl.when(has_earlier(d))
         def _():
             query_copy(d).start()
-    own_c = pltpu.make_async_copy(c_ref, c_all.at[me_t], c_loc)
+
+    def pump(c, s):
+        @pl.when(me_t >= s)
+        def _():
+            right_copy(c, s - 1).wait_recv()
+
+        if s < n_tensor - 1:
+            @pl.when(right_sends(s))
+            def _():
+                right_copy(c, s).start()
+
+        @pl.when(me_t + s < n_tensor)
+        def _():
+            left_copy(c, s - 1).wait_recv()
+
+        if s < n_tensor - 1:
+            @pl.when(left_sends(s))
+            def _():
+                left_copy(c, s).start()
+
+    pumped = []
+
+    def pump_next(count):
+        order = [(c, s) for s in range(1, min(3, n_tensor)) for c in range(chunks)]
+        order += [(c, s) for c in range(chunks) for s in range(3, n_tensor)]
+        for c, s in order[len(pumped) : len(pumped) + count]:
+            pump(c, s)
+            pumped.append((c, s))
+
+    own_c = pltpu.make_async_copy(c_ref, c_all.at[block(me_t)], c_loc)
     own_c.start()
     own_w = pltpu.make_async_copy(w_ref, w_all.at[me_f], w_loc)
     own_w.start()
@@ -164,6 +198,7 @@
             return jnp.where(j - i > d * rows - WINDOW, scores, masked_score)
         return scores
 
+    pump_next(1)
     lse_own[...] = jnp.zeros_like(lse_own)
     row_own[...] = jnp.zeros_like(row_own)
     for d in range(1, reach + 1):
@@ -203,20 +238,19 @@
                     part = dot(v_turn[kv, d], low)
                     turned[...] = part if d == 0 else turned[...] + part
                 on_earlier(d, spread)
-            att[h] = turned[...].T
+            att[h] = turned[...]
 
     for d in range(1, reach + 1):
         @pl.when(has_earlier(d))
         def _():
             lse_copy(d).start()
+
+    pump_next(1)
 
     own_w.wait()
     for o in range(1, n_fsdp):
         w_copy(o).wait_recv()
-    per_shard = fsdp_features // features
-    for t in range(n_tensor):
-        start = (t % per_shard) * features
-        w_cut[t] = w_all[t // per_shard, :, start : start + features]
+    pump_next(1)
 
     for d in range(1, reach + 1):
         @pl.when(has_later(d))
@@ -247,47 +281,26 @@
                 def _(kv):
                     for group in range(groups):
                         h = kv * groups + group
-                        g = g_in[d - 1, place, lanes(h)]
+                        g = g_in[d - 1, lanes(h), place]
                         probs = p_late[h, d - 1, :, place]
-                        slope = dot_nt(v_ref[:, lanes(kv)], g) - row_in[c, d - 1, pl.ds(h, 1), :]
+                        slope = dot(v_ref[:, lanes(kv)], g) - row_in[c, d - 1, pl.ds(h, 1), :]
                         low = (probs.astype(jnp.float32) * slope).astype(jnp.bfloat16)
                         dk_acc[kv] += dot(low, q_in[d - 1, place, lanes(h)])
-                        dv_acc[kv] += dot(probs, g)
+                        dv_acc[kv] += dot_nt(probs, g)
 
     for c in range(chunks):
         place = pl.ds(c * CHUNK, CHUNK)
-        sums = dot_nt(c_all[me_t, place], w_cut[me_t])
-        for s in range(1, n_tensor):
-            @pl.when(me_t >= s)
-            def _():
-                right_copy(c, s - 1).wait_recv()
-
-            if s < n_tensor - 1:
-                @pl.when(right_sends(s))
-                def _():
-                    right_copy(c, s).start()
-
-            @pl.when(me_t + s < n_tensor)
-            def _():
-                left_copy(c, s - 1).wait_recv()
-
-            if s < n_tensor - 1:
-                @pl.when(left_sends(s))
-                def _():
-                    left_copy(c, s).start()
-        for s in range(1, n_tensor):
-            slot = lax.rem(me_t + s, n_tensor)
-            sums += dot_nt(c_all[slot, place], w_cut[slot])
-        g_own[place] = sums.astype(jnp.bfloat16)
+        while not all((c, s) in pumped for s in range(1, n_tensor)):
+            pump_next(1)
+        sums = dot(w_all[0], c_all[:fsdp_features, place])
+        for f in range(1, n_fsdp):
+            sums += dot(w_all[f], c_all[f * fsdp_features : (f + 1) * fsdp_features, place])
+        g_own[:, place] = sums.astype(jnp.bfloat16)
 
         @pl.loop(0, kv_heads * groups)
         def _(h):
-            product = g_own[place, lanes(h)].astype(jnp.float32) * att[h, place]
-            row = lax.dot_general(
-                jnp.ones((8, HEAD_SIZE), jnp.float32), product, NT,
-                precision=lax.Precision.HIGHEST, preferred_element_type=jnp.float32,
-            )
-            row_own[c, pl.ds(h, 1), :] = row[0:1]
+            product = g_own[lanes(h), place].astype(jnp.float32) * att[h, :, place]
+            row_own[c, pl.ds(h, 1), :] = jnp.sum(product, axis=0, keepdims=True)
 
         for d in range(1, reach + 1):
             @pl.when(has_earlier(d))
@@ -299,18 +312,18 @@
         def _(kv):
             for group in range(groups):
                 h = kv * groups + group
-                g = g_own[place, lanes(h)]
+                g = g_own[lanes(h), place]
                 row = row_own[c, pl.ds(h, 1), :]
                 for d in range(reach + 1):
                     def query_part():
                         probs = p_own[h, d, :, place]
-                        slope = dot_nt(value_block(d)[:, lanes(kv)], g) - row
+                        slope = dot(value_block(d)[:, lanes(kv)], g) - row
                         low = (probs.astype(jnp.float32) * slope).astype(jnp.bfloat16)
                         part = dot(k_turn[kv, d], low)
                         if d == 0:
                             dq_acc[...] = part
                             dk_acc[kv] += dot(low, q_ref[place, lanes(h)])
-                            dv_acc[kv] += dot(probs, g)
+                            dv_acc[kv] += dot_nt(probs, g)
                         else:
                             dq_acc[...] += part
                     on_earlier(d, query_part)
@@ -350,9 +363,20 @@
                     copy.wait_send()
 
 
+def place_kernel(a_in, b_in, c_in, a_out, b_out, c_out, sems):
+    copies = [
+        pltpu.make_async_copy(src, dst, sems.at[i])
+        for i, (src, dst) in enumerate(((a_in, a_out), (b_in, b_out), (c_in, c_out)))
+    ]
+    for copy in copies:
+        copy.start()
+    for copy in copies:
+        copy.wait()
+
+
 def per_device(mesh, queries, keys, values, cotangent, out_weight):
     n_seq, n_tensor, n_fsdp = mesh.shape["seq"], mesh.shape["tensor"], mesh.shape["fsdp"]
-    q, k, v, c = queries[0], keys[0], values[0], cotangent[0]
+    q, k, v, c = queries[0], keys[0], values[0], cotangent[0].T
     rows = q.shape[0]
     reach = min(WINDOW // rows, n_seq - 1)
     heads, kv_heads = q.shape[1] // HEAD_SIZE, k.shape[1] // HEAD_SIZE
@@ -367,9 +391,8 @@
         in_specs=[vmem, vmem, vmem, hbm, hbm],
         out_specs=[vmem] * 3,
         scratch_shapes=[
-            pltpu.VMEM((n_tensor,) + c.shape, bf16),
+            pltpu.VMEM((n_tensor * c.shape[0], rows), bf16),
             pltpu.VMEM((n_fsdp,) + out_weight.shape, bf16),
-            pltpu.VMEM((n_tensor, out_weight.shape[0], c.shape[1]), bf16),
             pltpu.VMEM((reach,) + k.shape, bf16),
             pltpu.VMEM((reach,) + v.shape, bf16),
             pltpu.VMEM((reach,) + q.shape, bf16),
@@ -377,12 +400,12 @@
             pltpu.VMEM((reach, 8, rows), f32),
             pltpu.VMEM((chunks, 8, CHUNK), f32),
             pltpu.VMEM((chunks, reach, 8, CHUNK), f32),
-            pltpu.VMEM(q.shape, bf16),
-            pltpu.VMEM((reach,) + q.shape, bf16),
+            pltpu.VMEM(q.shape[::-1], bf16),
+            pltpu.VMEM((reach,) + q.shape[::-1], bf16),
             pltpu.VMEM((reach + 1, rows, rows), f32),
             pltpu.VMEM((heads, reach + 1, rows, rows), bf16),
             pltpu.VMEM((heads, reach, rows, rows), bf16),
-            pltpu.VMEM((heads, rows, HEAD_SIZE), f32),
+            pltpu.VMEM((heads, HEAD_SIZE, rows), f32),
             pltpu.VMEM((kv_heads, reach + 1, HEAD_SIZE, rows), bf16),
             pltpu.VMEM((kv_heads, reach + 1, HEAD_SIZE, rows), bf16),
             pltpu.VMEM((1, rows), f32),
@@ -404,6 +427,13 @@
         ),
         cost_estimate=pl.CostEstimate(flops=4 * 10**9, bytes_accessed=8 * 10**6, transcendentals=4 * 10**6),
     )(q, k, v, c, out_weight)
+    dq, dk, dv = pl.pallas_call(
+        place_kernel,
+        out_shape=[jax.ShapeDtypeStruct(x.shape, bf16) for x in (q, k, v)],
+        in_specs=[hbm] * 3,
+        out_specs=[hbm] * 3,
+        scratch_shapes=[dma((3,))],
+    )(dq, dk, dv)
     return dq[None], dk[None], dv[None]
 
 

time: 80.3 us -> 80.9 us (level)
  Pallas kernels: 72.3 us -> 80.1 us
  local copies, waits for them, and re-layouts: 7.04 us -> 0 us
    pallas_call x0 -> x1, Pallas kernels: none -> 17 us  [per_device(): pl.pallas_call(place_kernel, out_shape=[jax.ShapeDtypeStruct(x.shape, bf1...]
    pallas_call x1, Pallas kernels: 72.3 us -> 63 us  [per_device(): pl.pallas_call(functools.partial(kernel, n_seq, n_tensor, n_fsdp, reach),...]
    unnamed x4 -> x0, local copies, waits for them, and re-layouts: 7.04 us -> none
where the time goes in v2:
time: 80.9 us; the launch traced here: 80.7 us
  Pallas kernels  80.1 us (99%)
    pallas_call x1, Pallas kernels, per_device(): pl.pallas_call(functools.partial(kernel, n_seq, n_tensor, n_fsdp, reach),...  63 us
    pallas_call x1, Pallas kernels, per_device(): pl.pallas_call(place_kernel, out_shape=[jax.ShapeDtypeStruct(x.shape, bf1...  17 us

profile of v2, /device:TPU:0, one launch (start us, length us, event | category | flops | bytes accessed | tf_op | source)
XLA Modules:
  0.0 80.7 jit_solution(813206063714975020)
XLA Ops:
  0.6 63.0 %shard_map.76 = (bf16[256,512]{1,0:T(8,128)(2,1)}, bf16[256,256]{1,0:T(8,128)(2,1)}, bf16[256,256]{1,0:T(8,128)(2,1)}) custom-call(bf16[256,512]{1,0:T(8,128)(2,1)} %bitcast.10, bf16[256,256]{1,0:T(8,128)(2,1)} %bitcast.12, bf16[256,256]{1,0:T(8,128)(2,1)} %bitcast.13, bf16[1344,256]{1,0:T(8,128)(2,1)} %bitcast.9, bf16[512,2688]{1,0:T(8,128)(2,1)} %w_ref.1), custom_call_target="tpu_custom_call" | custom-call | flops 4000000000 | bytes 8000000 | tf_op jit(solution)/shard_map/pallas_call | solution.py:388
  63.7 17.0 %shard_map.77 = (bf16[256,512]{1,0:T(8,128)(2,1)}, bf16[256,256]{1,0:T(8,128)(2,1)}, bf16[256,256]{1,0:T(8,128)(2,1)}) custom-call(bf16[256,512]{1,0:T(8,128)(2,1)} %get-tuple-element.9.a_in, bf16[256,256]{1,0:T(8,128)(2,1)} %get-tuple-element.10.b_in, bf16[256,256]{1,0:T(8,128)(2,1)} %get-tuple-element.11.c_in), custom_call_target="tpu_custom_call" | custom-call | tf_op jit(solution)/shard_map/pallas_call | solution.py:430

commit v3 on v2

--- a/solution.py
+++ b/solution.py
@@ -25,14 +25,20 @@
     return lax.dot_general(a, b, NT, preferred_element_type=jnp.float32)
 
 
+def is_lean(n_seq, n_tensor, n_fsdp, reach):
+    return n_tensor == 4 and n_fsdp == 2 and n_seq > 1 and reach == n_seq - 1
+
+
 def kernel(
     n_seq, n_tensor, n_fsdp, reach,
     q_ref, k_ref, v_ref, c_ref, w_ref,
     dq_ref, dk_ref, dv_ref,
     c_all, w_all, k_in, v_in, q_in, lse_own, lse_in, row_own, row_in, g_own, g_in,
     s_buf, p_own, p_late, att, k_turn, v_turn, top, total, turned, dq_acc, dk_acc, dv_acc,
+    w_far, part_out, part_in,
     c_loc, w_loc, w_send, w_recv, right_send, right_recv, left_send, left_recv,
     kv_send, kv_recv, lse_send, lse_recv, g_send, g_recv,
+    far_send, far_recv, pass_send, pass_recv, part_send, part_recv,
 ):
     rows = q_ref.shape[0]
     kv_heads = k_ref.shape[1] // HEAD_SIZE
@@ -92,11 +98,54 @@
         src = c_ref.at[:, place] if s == 0 else there
         return remote(src, there, left_send.at[c, s], left_recv.at[c, s], tensor_at(-1))
 
+    lean = is_lean(n_seq, n_tensor, n_fsdp, reach)
+    is_end = (me_t == 0) | (me_t == 3)
+    is_helper = (me_t == 1) | (me_t == 2)
+    far_shard = 1 - lax.div(me_t, 2)
+    gives_far = is_end & (me_f == far_shard)
+    holds_far = is_helper & (me_f == far_shard)
+    takes_far = is_helper & (me_f != far_shard)
+
+    def far_rows(offset):
+        quarter = w_ref.shape[0] // n_seq
+        piece = lax.rem(me_s - offset + n_seq, n_seq)
+        return pl.ds(pl.multiple_of(piece * quarter, 16), quarter)
+
+    def far_first():
+        place = far_rows(0)
+        return remote(w_ref.at[place], w_far.at[place], far_send.at[0], far_recv.at[0],
+                      {"tensor": 1 + lax.div(me_t, 3)})
+
+    def far_share(d):
+        place = far_rows(0)
+        return remote(w_far.at[place], w_far.at[place], far_send.at[d], far_recv.at[d], seq_at(d))
+
+    def far_pass(d):
+        place = far_rows(d)
+        return remote(w_far.at[place], w_far.at[place], pass_send.at[d], pass_recv.at[d], fsdp_at(1))
+
+    def part_copy(c):
+        place = pl.ds(c * CHUNK, CHUNK)
+        return remote(part_out.at[:, place], part_in.at[:, place], part_send.at[c], part_recv.at[c],
+                      {"tensor": 3 * lax.div(me_t, 2)})
+
     def right_sends(s):
+        if lean and s > 0:
+            return me_t == 1
         return (me_t + 1 < n_tensor) & (me_t >= s)
 
     def left_sends(s):
+        if lean and s > 0:
+            return me_t == 2
         return (me_t >= 1) & (me_t + s < n_tensor)
+
+    def right_lands(s):
+        return me_t == 2 if lean and s > 1 else me_t >= s
+
+    def left_lands(s):
+        return me_t == 1 if lean and s > 1 else me_t + s < n_tensor
+
+    hops = 3 if lean else n_tensor
 
     def w_copy(o):
         return remote(w_ref, w_all.at[me_f], w_send.at[o], w_recv.at[o], fsdp_at(o))
@@ -128,6 +177,11 @@
         @pl.when(left_sends(0))
         def _():
             left_copy(c, 0).start()
+
+        if lean and c == 0:
+            @pl.when(gives_far)
+            def _():
+                far_first().start()
     for o in range(1, n_fsdp):
         w_copy(o).start()
     for d in range(1, reach + 1):
@@ -141,20 +195,20 @@
             query_copy(d).start()
 
     def pump(c, s):
-        @pl.when(me_t >= s)
+        @pl.when(right_lands(s))
         def _():
             right_copy(c, s - 1).wait_recv()
 
-        if s < n_tensor - 1:
+        if s < hops - 1:
             @pl.when(right_sends(s))
             def _():
                 right_copy(c, s).start()
 
-        @pl.when(me_t + s < n_tensor)
+        @pl.when(left_lands(s))
         def _():
             left_copy(c, s - 1).wait_recv()
 
-        if s < n_tensor - 1:
+        if s < hops - 1:
             @pl.when(left_sends(s))
             def _():
                 left_copy(c, s).start()
@@ -162,8 +216,8 @@
     pumped = []
 
     def pump_next(count):
-        order = [(c, s) for s in range(1, min(3, n_tensor)) for c in range(chunks)]
-        order += [(c, s) for c in range(chunks) for s in range(3, n_tensor)]
+        order = [(c, s) for s in range(1, min(3, hops)) for c in range(chunks)]
+        order += [(c, s) for c in range(chunks) for s in range(3, hops)]
         for c, s in order[len(pumped) : len(pumped) + count]:
             pump(c, s)
             pumped.append((c, s))
@@ -247,6 +301,14 @@
 
     pump_next(1)
 
+    if lean:
+        @pl.when(holds_far)
+        def _():
+            far_first().wait_recv()
+            for d in range(1, n_seq):
+                far_share(d).start()
+            far_pass(0).start()
+
     own_w.wait()
     for o in range(1, n_fsdp):
         w_copy(o).wait_recv()
@@ -264,6 +326,18 @@
                     h = kv * groups + group
                     scores = masked(dot_nt(k_ref[:, lanes(kv)], q_in[d - 1, :, lanes(h)]) * score_scale, d)
                     p_late[h, d - 1] = jnp.exp(scores - lse_in[d - 1, pl.ds(h, 1), :]).astype(jnp.bfloat16)
+
+    if lean:
+        @pl.when(holds_far)
+        def _():
+            for d in range(1, n_seq):
+                far_share(d).wait_recv()
+                far_pass(d).start()
+
+        @pl.when(takes_far)
+        def _():
+            for d in range(n_seq):
+                far_pass(d).wait_recv()
 
     dk_acc[...] = jnp.zeros_like(dk_acc)
     dv_acc[...] = jnp.zeros_like(dv_acc)
@@ -290,12 +364,33 @@
 
     for c in range(chunks):
         place = pl.ds(c * CHUNK, CHUNK)
-        while not all((c, s) in pumped for s in range(1, n_tensor)):
+        while not all((c, s) in pumped for s in range(1, hops)):
             pump_next(1)
-        sums = dot(w_all[0], c_all[:fsdp_features, place])
-        for f in range(1, n_fsdp):
-            sums += dot(w_all[f], c_all[f * fsdp_features : (f + 1) * fsdp_features, place])
-        g_own[:, place] = sums.astype(jnp.bfloat16)
+        def full_sums():
+            sums = dot(w_all[0], c_all[:fsdp_features, place])
+            for f in range(1, n_fsdp):
+                sums += dot(w_all[f], c_all[f * fsdp_features : (f + 1) * fsdp_features, place])
+            g_own[:, place] = sums.astype(jnp.bfloat16)
+
+        def shard_features(f):
+            return pl.ds(pl.multiple_of(f * fsdp_features, 16), fsdp_features)
+
+        if lean:
+            @pl.when(is_helper)
+            def _():
+                part = dot(w_far[...], c_all[shard_features(far_shard), place])
+                part_out[:, place] = part.astype(jnp.bfloat16)
+                part_copy(c).start()
+                full_sums()
+
+            @pl.when(is_end)
+            def _():
+                near = 1 - far_shard
+                sums = dot(w_all[near], c_all[shard_features(near), place])
+                part_copy(c).wait_recv()
+                g_own[:, place] = (sums + part_in[:, place].astype(jnp.float32)).astype(jnp.bfloat16)
+        else:
+            full_sums()
 
         @pl.loop(0, kv_heads * groups)
         def _(h):
@@ -339,8 +434,25 @@
 
     for o in range(1, n_fsdp):
         w_copy(o).wait_send()
+    if lean:
+        @pl.when(gives_far)
+        def _():
+            far_first().wait_send()
+
+        @pl.when(holds_far)
+        def _():
+            for d in range(1, n_seq):
+                far_share(d).wait_send()
+            for d in range(n_seq):
+                far_pass(d).wait_send()
+
+        @pl.when(is_helper)
+        def _():
+            for c in range(chunks):
+                part_copy(c).wait_send()
+
     for c in range(chunks):
-        for s in range(n_tensor - 1):
+        for s in range(hops - 1):
             @pl.when(right_sends(s))
             def _():
                 right_copy(c, s).wait_send()
@@ -379,6 +491,7 @@
     q, k, v, c = queries[0], keys[0], values[0], cotangent[0].T
     rows = q.shape[0]
     reach = min(WINDOW // rows, n_seq - 1)
+    lean = is_lean(n_seq, n_tensor, n_fsdp, reach)
     heads, kv_heads = q.shape[1] // HEAD_SIZE, k.shape[1] // HEAD_SIZE
     chunks = rows // CHUNK
     bf16, f32 = jnp.bfloat16, jnp.float32
@@ -414,6 +527,9 @@
             pltpu.VMEM((HEAD_SIZE, CHUNK), f32),
             pltpu.VMEM((kv_heads, rows, HEAD_SIZE), f32),
             pltpu.VMEM((kv_heads, rows, HEAD_SIZE), f32),
+            pltpu.VMEM(out_weight.shape if lean else (16, 128), bf16),
+            pltpu.VMEM((out_weight.shape[0], rows) if lean else (16, 128), bf16),
+            pltpu.VMEM((out_weight.shape[0], rows) if lean else (16, 128), bf16),
             dma, dma,
             dma((n_fsdp,)), dma((n_fsdp,)),
             dma((chunks, n_tensor)), dma((chunks, n_tensor)),
@@ -421,6 +537,7 @@
             dma((3, reach + 1)), dma((3, reach + 1)),
             dma((reach + 1,)), dma((reach + 1,)),
             dma((2, chunks, reach + 1)), dma((2, chunks, reach + 1)),
+            dma((n_seq,)), dma((n_seq,)), dma((n_seq,)), dma((n_seq,)), dma((chunks,)), dma((chunks,)),
         ],
         compiler_params=pltpu.CompilerParams(
             collective_id=0, has_side_effects=True, vmem_limit_bytes=56 * 2**20
@@ -430,7 +547,7 @@
     dq, dk, dv = pl.pallas_call(
         place_kernel,
         out_shape=[jax.ShapeDtypeStruct(x.shape, bf16) for x in (q, k, v)],
-        in_specs=[hbm] * 3,
+        in_specs=[vmem] * 3,
         out_specs=[hbm] * 3,
         scratch_shapes=[dma((3,))],
     )(dq, dk, dv)

time: 80.9 us -> 75.7 us (0.936)
  Pallas kernels: 80.1 us -> 74.9 us
    pallas_call x1, Pallas kernels: 17 us -> 1.86 us  [per_device(): pl.pallas_call(place_kernel, out_shape=[jax.ShapeDtypeStruct(x.shape, bf1...]
    pallas_call x1, Pallas kernels: 63 us -> 73 us  [per_device(): pl.pallas_call(functools.partial(kernel, n_seq, n_tensor, n_fsdp, reach),...]
where the time goes in v3:
time: 75.7 us; the launch traced here: 75.5 us
  Pallas kernels  74.9 us (99%)
    pallas_call x1, Pallas kernels, per_device(): pl.pallas_call(functools.partial(kernel, n_seq, n_tensor, n_fsdp, reach),...  73 us
    pallas_call x1, Pallas kernels, per_device(): pl.pallas_call(place_kernel, out_shape=[jax.ShapeDtypeStruct(x.shape, bf1...  1.86 us

profile of v3, /device:TPU:0, one launch (start us, length us, event | category | flops | bytes accessed | tf_op | source)
XLA Modules:
  0.0 75.5 jit_solution(267104634968172613)
XLA Ops:
  0.6 73.0 %shard_map.76 = (bf16[256,512]{1,0:T(8,128)(2,1)}, bf16[256,256]{1,0:T(8,128)(2,1)}, bf16[256,256]{1,0:T(8,128)(2,1)}) custom-call(bf16[256,512]{1,0:T(8,128)(2,1)} %bitcast.10, bf16[256,256]{1,0:T(8,128)(2,1)} %bitcast.12, bf16[256,256]{1,0:T(8,128)(2,1)} %bitcast.13, bf16[1344,256]{1,0:T(8,128)(2,1)} %bitcast.9, bf16[512,2688]{1,0:T(8,128)(2,1)} %w_ref.1), custom_call_target="tpu_custom_call" | custom-call | flops 4000000000 | bytes 8000000 | tf_op jit(solution)/shard_map/pallas_call | solution.py:501
  73.7 1.9 %shard_map.77 = (bf16[256,512]{1,0:T(8,128)(2,1)}, bf16[256,256]{1,0:T(8,128)(2,1)}, bf16[256,256]{1,0:T(8,128)(2,1)}) custom-call(bf16[256,512]{1,0:T(8,128)(2,1)} %get-tuple-element.9.a_in, bf16[256,256]{1,0:T(8,128)(2,1)} %get-tuple-element.10.b_in, bf16[256,256]{1,0:T(8,128)(2,1)} %get-tuple-element.11.c_in), custom_call_target="tpu_custom_call" | custom-call | tf_op jit(solution)/shard_map/pallas_call | solution.py:547

commit v4 on v3

--- a/solution.py
+++ b/solution.py
@@ -26,7 +26,7 @@
 
 
 def is_lean(n_seq, n_tensor, n_fsdp, reach):
-    return n_tensor == 4 and n_fsdp == 2 and n_seq > 1 and reach == n_seq - 1
+    return False
 
 
 def kernel(
@@ -34,7 +34,7 @@
     q_ref, k_ref, v_ref, c_ref, w_ref,
     dq_ref, dk_ref, dv_ref,
     c_all, w_all, k_in, v_in, q_in, lse_own, lse_in, row_own, row_in, g_own, g_in,
-    s_buf, p_own, p_late, att, k_turn, v_turn, top, total, turned, dq_acc, dk_acc, dv_acc,
+    s_buf, p_own, p_late, att, k_turn, v_turn, top, total, dq_acc, dk_acc, dv_acc,
     w_far, part_out, part_in,
     c_loc, w_loc, w_send, w_recv, right_send, right_recv, left_send, left_recv,
     kv_send, kv_recv, lse_send, lse_recv, g_send, g_recv,
@@ -43,6 +43,7 @@
     rows = q_ref.shape[0]
     kv_heads = k_ref.shape[1] // HEAD_SIZE
     groups = q_ref.shape[1] // k_ref.shape[1]
+    heads = kv_heads * groups
     chunks = rows // CHUNK
     features = c_ref.shape[0]
     fsdp_features = w_ref.shape[1]
@@ -228,7 +229,7 @@
     own_w.start()
 
     def lanes(h):
-        return pl.ds(pl.multiple_of(h * HEAD_SIZE, HEAD_SIZE), HEAD_SIZE)
+        return slice(h * HEAD_SIZE, (h + 1) * HEAD_SIZE)
 
     def key_block(d):
         return k_ref if d == 0 else k_in.at[d - 1]
@@ -261,45 +262,40 @@
             for copy in key_copies(d):
                 copy.wait_recv()
 
-    @pl.loop(0, kv_heads)
-    def _(kv):
-        for d in range(reach + 1):
-            def turn():
+    for d in range(reach + 1):
+        def score():
+            for kv in range(kv_heads):
                 k_turn[kv, d] = key_block(d)[:, lanes(kv)].T
                 v_turn[kv, d] = value_block(d)[:, lanes(kv)].T
-            on_earlier(d, turn)
-        for group in range(groups):
-            h = kv * groups + group
-            q = q_ref[:, lanes(h)]
-            for d in range(reach + 1):
-                def score():
-                    scores = masked(dot_nt(key_block(d)[:, lanes(kv)], q) * score_scale, d)
-                    s_buf[d] = scores
-                    high = jnp.max(scores, axis=0, keepdims=True)
-                    top[...] = high if d == 0 else jnp.maximum(top[...], high)
-                on_earlier(d, score)
-            for d in range(reach + 1):
-                def add():
-                    part = jnp.sum(jnp.exp(s_buf[d] - top[...]), axis=0, keepdims=True)
-                    total[...] = part if d == 0 else total[...] + part
-                on_earlier(d, add)
-            lse = top[...] + jnp.log(total[...])
-            lse_own[pl.ds(h, 1), :] = lse
-            for d in range(reach + 1):
-                def spread():
-                    low = jnp.exp(s_buf[d] - lse_own[pl.ds(h, 1), :]).astype(jnp.bfloat16)
-                    p_own[h, d] = low
-                    part = dot(v_turn[kv, d], low)
-                    turned[...] = part if d == 0 else turned[...] + part
-                on_earlier(d, spread)
-            att[h] = turned[...]
-
+            for h in range(heads):
+                scores = masked(dot_nt(key_block(d)[:, lanes(h // groups)], q_ref[:, lanes(h)]) * score_scale, d)
+                s_buf[h, d] = scores
+                high = jnp.max(scores, axis=0, keepdims=True)
+                top[h] = high if d == 0 else jnp.maximum(top[h], high)
+        on_earlier(d, score)
+    pump_next(1)
+    for d in range(reach + 1):
+        def add():
+            for h in range(heads):
+                powers = jnp.exp(s_buf[h, d] - top[h])
+                part = jnp.sum(powers, axis=0, keepdims=True)
+                total[h] = part if d == 0 else total[h] + part
+        on_earlier(d, add)
+    for h in range(heads):
+        lse_own[h : h + 1, :] = top[h] + jnp.log(total[h])
     for d in range(1, reach + 1):
         @pl.when(has_earlier(d))
         def _():
             lse_copy(d).start()
 
-    pump_next(1)
+    for d in range(reach + 1):
+        def spread():
+            for h in range(heads):
+                low = jnp.exp(s_buf[h, d] - lse_own[h : h + 1, :]).astype(jnp.bfloat16)
+                p_own[h, d] = low
+                part = dot(v_turn[h // groups, d], low)
+                att[h] = part if d == 0 else att[h] + part
+        on_earlier(d, spread)
 
     if lean:
         @pl.when(holds_far)
@@ -320,12 +316,9 @@
             query_copy(d).wait_recv()
             lse_copy(d).wait_recv()
 
-            @pl.loop(0, kv_heads)
-            def _(kv):
-                for group in range(groups):
-                    h = kv * groups + group
-                    scores = masked(dot_nt(k_ref[:, lanes(kv)], q_in[d - 1, :, lanes(h)]) * score_scale, d)
-                    p_late[h, d - 1] = jnp.exp(scores - lse_in[d - 1, pl.ds(h, 1), :]).astype(jnp.bfloat16)
+            for h in range(heads):
+                scores = masked(dot_nt(k_ref[:, lanes(h // groups)], q_in[d - 1, :, lanes(h)]) * score_scale, d)
+                p_late[h, d - 1] = jnp.exp(scores - lse_in[d - 1, h : h + 1, :]).astype(jnp.bfloat16)
 
     if lean:
         @pl.when(holds_far)
@@ -351,19 +344,21 @@
                 for copy in grad_copies(c, d):
                     copy.wait_recv()
 
-                @pl.loop(0, kv_heads)
-                def _(kv):
-                    for group in range(groups):
-                        h = kv * groups + group
+                for kv in range(kv_heads):
+                    k_part, v_part = dk_acc[kv], dv_acc[kv]
+                    for h in range(kv * groups, (kv + 1) * groups):
                         g = g_in[d - 1, lanes(h), place]
                         probs = p_late[h, d - 1, :, place]
-                        slope = dot(v_ref[:, lanes(kv)], g) - row_in[c, d - 1, pl.ds(h, 1), :]
+                        slope = dot(v_ref[:, lanes(kv)], g) - row_in[c, d - 1, h : h + 1, :]
                         low = (probs.astype(jnp.float32) * slope).astype(jnp.bfloat16)
-                        dk_acc[kv] += dot(low, q_in[d - 1, place, lanes(h)])
-                        dv_acc[kv] += dot_nt(probs, g)
+                        k_part += dot(low, q_in[d - 1, place, lanes(h)])
+                        v_part += dot_nt(probs, g)
+                    dk_acc[kv], dv_acc[kv] = k_part, v_part
 
     for c in range(chunks):
         place = pl.ds(c * CHUNK, CHUNK)
+        if c > 0:
+            late_keys(c - 1)
         while not all((c, s) in pumped for s in range(1, hops)):
             pump_next(1)
         def full_sums():
@@ -392,10 +387,9 @@
         else:
             full_sums()
 
-        @pl.loop(0, kv_heads * groups)
-        def _(h):
+        for h in range(heads):
             product = g_own[lanes(h), place].astype(jnp.float32) * att[h, :, place]
-            row_own[c, pl.ds(h, 1), :] = jnp.sum(product, axis=0, keepdims=True)
+            row_own[c, h : h + 1, :] = jnp.sum(product, axis=0, keepdims=True)
 
         for d in range(1, reach + 1):
             @pl.when(has_earlier(d))
@@ -403,29 +397,25 @@
                 for copy in grad_copies(c, d):
                     copy.start()
 
-        @pl.loop(0, kv_heads)
-        def _(kv):
-            for group in range(groups):
-                h = kv * groups + group
-                g = g_own[lanes(h), place]
-                row = row_own[c, pl.ds(h, 1), :]
-                for d in range(reach + 1):
-                    def query_part():
+        for d in range(reach + 1):
+            def query_part():
+                for kv in range(kv_heads):
+                    for h in range(kv * groups, (kv + 1) * groups):
+                        g = g_own[lanes(h), place]
                         probs = p_own[h, d, :, place]
-                        slope = dot(value_block(d)[:, lanes(kv)], g) - row
+                        slope = dot(value_block(d)[:, lanes(kv)], g) - row_own[c, h : h + 1, :]
                         low = (probs.astype(jnp.float32) * slope).astype(jnp.bfloat16)
                         part = dot(k_turn[kv, d], low)
                         if d == 0:
-                            dq_acc[...] = part
+                            dq_acc[h] = part
                             dk_acc[kv] += dot(low, q_ref[place, lanes(h)])
                             dv_acc[kv] += dot_nt(probs, g)
                         else:
-                            dq_acc[...] += part
-                    on_earlier(d, query_part)
-                dq_ref[place, lanes(h)] = (dq_acc[...] * score_scale).T.astype(jnp.bfloat16)
-
-        if c > 0:
-            late_keys(c - 1)
+                            dq_acc[h] += part
+            on_earlier(d, query_part)
+        for h in range(heads):
+            dq_ref[place, lanes(h)] = (dq_acc[h] * score_scale).T.astype(jnp.bfloat16)
+
     late_keys(chunks - 1)
     for kv in range(kv_heads):
         lane = slice(kv * HEAD_SIZE, (kv + 1) * HEAD_SIZE)
@@ -515,16 +505,15 @@
             pltpu.VMEM((chunks, reach, 8, CHUNK), f32),
             pltpu.VMEM(q.shape[::-1], bf16),
             pltpu.VMEM((reach,) + q.shape[::-1], bf16),
-            pltpu.VMEM((reach + 1, rows, rows), f32),
+            pltpu.VMEM((heads, reach + 1, rows, rows), f32),
             pltpu.VMEM((heads, reach + 1, rows, rows), bf16),
             pltpu.VMEM((heads, reach, rows, rows), bf16),
             pltpu.VMEM((heads, HEAD_SIZE, rows), f32),
             pltpu.VMEM((kv_heads, reach + 1, HEAD_SIZE, rows), bf16),
             pltpu.VMEM((kv_heads, reach + 1, HEAD_SIZE, rows), bf16),
-            pltpu.VMEM((1, rows), f32),
-            pltpu.VMEM((1, rows), f32),
-            pltpu.VMEM((HEAD_SIZE, rows), f32),
-            pltpu.VMEM((HEAD_SIZE, CHUNK), f32),
+            pltpu.VMEM((heads, 1, rows), f32),
+            pltpu.VMEM((heads, 1, rows), f32),
+            pltpu.VMEM((heads, HEAD_SIZE, CHUNK), f32),
             pltpu.VMEM((kv_heads, rows, HEAD_SIZE), f32),
             pltpu.VMEM((kv_heads, rows, HEAD_SIZE), f32),
             pltpu.VMEM(out_weight.shape if lean else (16, 128), bf16),

time: 75.7 us -> 65.5 us (0.87)
  Pallas kernels: 74.9 us -> 64.7 us
    pallas_call x1, Pallas kernels: 73 us -> 62.9 us  [per_device(): pl.pallas_call(functools.partial(kernel, n_seq, n_tensor, n_fsdp, reach),...]
where the time goes in v4:
time: 65.5 us; the launch traced here: 65.3 us
  Pallas kernels  64.7 us (99%)
    pallas_call x1, Pallas kernels, per_device(): pl.pallas_call(functools.partial(kernel, n_seq, n_tensor, n_fsdp, reach),...  62.9 us
    pallas_call x1, Pallas kernels, per_device(): pl.pallas_call(place_kernel, out_shape=[jax.ShapeDtypeStruct(x.shape, bf1...  1.86 us

profile of v4, /device:TPU:0, one launch (start us, length us, event | category | flops | bytes accessed | tf_op | source)
XLA Modules:
  0.0 65.3 jit_solution(15856707842478654423)
XLA Ops:
  0.6 62.9 %shard_map.76 = (bf16[256,512]{1,0:T(8,128)(2,1)}, bf16[256,256]{1,0:T(8,128)(2,1)}, bf16[256,256]{1,0:T(8,128)(2,1)}) custom-call(bf16[256,512]{1,0:T(8,128)(2,1)} %bitcast.10, bf16[256,256]{1,0:T(8,128)(2,1)} %bitcast.12, bf16[256,256]{1,0:T(8,128)(2,1)} %bitcast.13, bf16[1344,256]{1,0:T(8,128)(2,1)} %bitcast.9, bf16[512,2688]{1,0:T(8,128)(2,1)} %w_ref.1), custom_call_target="tpu_custom_call" | custom-call | flops 4000000000 | bytes 8000000 | tf_op jit(solution)/shard_map/pallas_call | solution.py:491
  63.5 1.9 %shard_map.77 = (bf16[256,512]{1,0:T(8,128)(2,1)}, bf16[256,256]{1,0:T(8,128)(2,1)}, bf16[256,256]{1,0:T(8,128)(2,1)}) custom-call(bf16[256,512]{1,0:T(8,128)(2,1)} %get-tuple-element.9.a_in, bf16[256,256]{1,0:T(8,128)(2,1)} %get-tuple-element.10.b_in, bf16[256,256]{1,0:T(8,128)(2,1)} %get-tuple-element.11.c_in), custom_call_target="tpu_custom_call" | custom-call | tf_op jit(solution)/shard_map/pallas_call | solution.py:536

commit v5 on v4

--- a/solution.py
+++ b/solution.py
@@ -253,7 +253,7 @@
             return jnp.where(j - i > d * rows - WINDOW, scores, masked_score)
         return scores
 
-    pump_next(1)
+    pump_next(chunks)
     lse_own[...] = jnp.zeros_like(lse_own)
     row_own[...] = jnp.zeros_like(row_own)
     for d in range(1, reach + 1):
@@ -273,7 +273,6 @@
                 high = jnp.max(scores, axis=0, keepdims=True)
                 top[h] = high if d == 0 else jnp.maximum(top[h], high)
         on_earlier(d, score)
-    pump_next(1)
     for d in range(reach + 1):
         def add():
             for h in range(heads):
@@ -332,6 +331,7 @@
             for d in range(n_seq):
                 far_pass(d).wait_recv()
 
+    pump_next(1)
     dk_acc[...] = jnp.zeros_like(dk_acc)
     dv_acc[...] = jnp.zeros_like(dv_acc)
     own_c.wait()

time: 65.5 us -> 65.5 us (level)
  no operation moved by 1% of the time
where the time goes in v5:
time: 65.5 us; the launch traced here: 65.3 us
  Pallas kernels  64.7 us (99%)
    pallas_call x1, Pallas kernels, per_device(): pl.pallas_call(functools.partial(kernel, n_seq, n_tensor, n_fsdp, reach),...  62.9 us
    pallas_call x1, Pallas kernels, per_device(): pl.pallas_call(place_kernel, out_shape=[jax.ShapeDtypeStruct(x.shape, bf1...  1.86 us

profile of v5, /device:TPU:0, one launch (start us, length us, event | category | flops | bytes accessed | tf_op | source)
XLA Modules:
  0.0 65.3 jit_solution(15189779735324398221)
XLA Ops:
  0.6 62.9 %shard_map.76 = (bf16[256,512]{1,0:T(8,128)(2,1)}, bf16[256,256]{1,0:T(8,128)(2,1)}, bf16[256,256]{1,0:T(8,128)(2,1)}) custom-call(bf16[256,512]{1,0:T(8,128)(2,1)} %bitcast.10, bf16[256,256]{1,0:T(8,128)(2,1)} %bitcast.12, bf16[256,256]{1,0:T(8,128)(2,1)} %bitcast.13, bf16[1344,256]{1,0:T(8,128)(2,1)} %bitcast.9, bf16[512,2688]{1,0:T(8,128)(2,1)} %w_ref.1), custom_call_target="tpu_custom_call" | custom-call | flops 4000000000 | bytes 8000000 | tf_op jit(solution)/shard_map/pallas_call | solution.py:491
  63.5 1.9 %shard_map.77 = (bf16[256,512]{1,0:T(8,128)(2,1)}, bf16[256,256]{1,0:T(8,128)(2,1)}, bf16[256,256]{1,0:T(8,128)(2,1)}) custom-call(bf16[256,512]{1,0:T(8,128)(2,1)} %get-tuple-element.9.a_in, bf16[256,256]{1,0:T(8,128)(2,1)} %get-tuple-element.10.b_in, bf16[256,256]{1,0:T(8,128)(2,1)} %get-tuple-element.11.c_in), custom_call_target="tpu_custom_call" | custom-call | tf_op jit(solution)/shard_map/pallas_call | solution.py:536

commit v6 on v5

--- a/solution.py
+++ b/solution.py
@@ -26,7 +26,7 @@
 
 
 def is_lean(n_seq, n_tensor, n_fsdp, reach):
-    return False
+    return n_tensor == 4 and n_fsdp == 2 and n_seq > 1 and reach == n_seq - 1
 
 
 def kernel(
@@ -170,6 +170,11 @@
             remote(row_own.at[c], row_in.at[c, d - 1], g_send.at[1, c, d], g_recv.at[1, c, d], seq_at(-d)),
         ]
 
+    if lean:
+        @pl.when(gives_far)
+        def _():
+            far_first().start()
+
     for c in range(chunks):
         @pl.when(right_sends(0))
         def _():
@@ -178,11 +183,6 @@
         @pl.when(left_sends(0))
         def _():
             left_copy(c, 0).start()
-
-        if lean and c == 0:
-            @pl.when(gives_far)
-            def _():
-                far_first().start()
     for o in range(1, n_fsdp):
         w_copy(o).start()
     for d in range(1, reach + 1):
@@ -252,6 +252,14 @@
             j, i = lax.broadcasted_iota(jnp.int32, shape, 0), lax.broadcasted_iota(jnp.int32, shape, 1)
             return jnp.where(j - i > d * rows - WINDOW, scores, masked_score)
         return scores
+
+    if lean:
+        @pl.when(holds_far)
+        def _():
+            far_first().wait_recv()
+            for d in range(1, n_seq):
+                far_share(d).start()
+            far_pass(0).start()
 
     pump_next(chunks)
     lse_own[...] = jnp.zeros_like(lse_own)
@@ -287,6 +295,13 @@
         def _():
             lse_copy(d).start()
 
+    if lean:
+        @pl.when(holds_far)
+        def _():
+            for d in range(1, n_seq):
+                far_share(d).wait_recv()
+                far_pass(d).start()
+
     for d in range(reach + 1):
         def spread():
             for h in range(heads):
@@ -296,14 +311,6 @@
                 att[h] = part if d == 0 else att[h] + part
         on_earlier(d, spread)
 
-    if lean:
-        @pl.when(holds_far)
-        def _():
-            far_first().wait_recv()
-            for d in range(1, n_seq):
-                far_share(d).start()
-            far_pass(0).start()
-
     own_w.wait()
     for o in range(1, n_fsdp):
         w_copy(o).wait_recv()
@@ -320,18 +327,13 @@
                 p_late[h, d - 1] = jnp.exp(scores - lse_in[d - 1, h : h + 1, :]).astype(jnp.bfloat16)
 
     if lean:
-        @pl.when(holds_far)
-        def _():
-            for d in range(1, n_seq):
-                far_share(d).wait_recv()
-                far_pass(d).start()
-
         @pl.when(takes_far)
         def _():
             for d in range(n_seq):
                 far_pass(d).wait_recv()
 
-    pump_next(1)
+    if not lean:
+        pump_next(1)
     dk_acc[...] = jnp.zeros_like(dk_acc)
     dv_acc[...] = jnp.zeros_like(dv_acc)
     own_c.wait()

time: 65.5 us -> 70.1 us (1.070); the launches traced: 65.3 us -> 68.8 us
  Pallas kernels: 64.7 us -> 68 us
    pallas_call x1, Pallas kernels: 62.9 us -> 66.1 us  [per_device(): pl.pallas_call(functools.partial(kernel, n_seq, n_tensor, n_fsdp, reach),...]
where the time goes in v6:
time: 70.1 us; the launch traced here: 68.8 us
  Pallas kernels  68 us (97%)
  between operations  0.8 us (1%)
    pallas_call x1, Pallas kernels, per_device(): pl.pallas_call(functools.partial(kernel, n_seq, n_tensor, n_fsdp, reach),...  66.1 us
    pallas_call x1, Pallas kernels, per_device(): pl.pallas_call(place_kernel, out_shape=[jax.ShapeDtypeStruct(x.shape, bf1...  1.86 us

profile of v6, /device:TPU:0, one launch (start us, length us, event | category | flops | bytes accessed | tf_op | source)
XLA Modules:
  0.0 68.8 jit_solution(17384686989145899401)
XLA Ops:
  0.6 66.1 %shard_map.76 = (bf16[256,512]{1,0:T(8,128)(2,1)}, bf16[256,256]{1,0:T(8,128)(2,1)}, bf16[256,256]{1,0:T(8,128)(2,1)}) custom-call(bf16[256,512]{1,0:T(8,128)(2,1)} %bitcast.10, bf16[256,256]{1,0:T(8,128)(2,1)} %bitcast.12, bf16[256,256]{1,0:T(8,128)(2,1)} %bitcast.13, bf16[1344,256]{1,0:T(8,128)(2,1)} %bitcast.9, bf16[512,2688]{1,0:T(8,128)(2,1)} %w_ref.1), custom_call_target="tpu_custom_call" | custom-call | flops 4000000000 | bytes 8000000 | tf_op jit(solution)/shard_map/pallas_call | solution.py:493
  66.8 1.9 %shard_map.77 = (bf16[256,512]{1,0:T(8,128)(2,1)}, bf16[256,256]{1,0:T(8,128)(2,1)}, bf16[256,256]{1,0:T(8,128)(2,1)}) custom-call(bf16[256,512]{1,0:T(8,128)(2,1)} %get-tuple-element.9.a_in, bf16[256,256]{1,0:T(8,128)(2,1)} %get-tuple-element.10.b_in, bf16[256,256]{1,0:T(8,128)(2,1)} %get-tuple-element.11.c_in), custom_call_target="tpu_custom_call" | custom-call | tf_op jit(solution)/shard_map/pallas_call | solution.py:538

commit v7 on v4

--- a/solution.py
+++ b/solution.py
@@ -88,14 +88,14 @@
     def right_copy(c, s):
         place = pl.ds(c * CHUNK, CHUNK)
         slot = lax.rem(me_t - s + n_tensor, n_tensor)
-        there = c_all.at[block(slot), place]
+        there = c_all.at[c, block(slot)]
         src = c_ref.at[:, place] if s == 0 else there
         return remote(src, there, right_send.at[c, s], right_recv.at[c, s], tensor_at(1))
 
     def left_copy(c, s):
         place = pl.ds(c * CHUNK, CHUNK)
         slot = lax.rem(me_t + s, n_tensor)
-        there = c_all.at[block(slot), place]
+        there = c_all.at[c, block(slot)]
         src = c_ref.at[:, place] if s == 0 else there
         return remote(src, there, left_send.at[c, s], left_recv.at[c, s], tensor_at(-1))
 
@@ -223,8 +223,12 @@
             pump(c, s)
             pumped.append((c, s))
 
-    own_c = pltpu.make_async_copy(c_ref, c_all.at[block(me_t)], c_loc)
-    own_c.start()
+    own_c = [
+        pltpu.make_async_copy(c_ref.at[:, pl.ds(c * CHUNK, CHUNK)], c_all.at[c, block(me_t)], c_loc.at[c])
+        for c in range(chunks)
+    ]
+    for copy in own_c:
+        copy.start()
     own_w = pltpu.make_async_copy(w_ref, w_all.at[me_f], w_loc)
     own_w.start()
 
@@ -334,7 +338,8 @@
 
     dk_acc[...] = jnp.zeros_like(dk_acc)
     dv_acc[...] = jnp.zeros_like(dv_acc)
-    own_c.wait()
+    for copy in own_c:
+        copy.wait()
 
     def late_keys(c):
         place = pl.ds(c * CHUNK, CHUNK)
@@ -362,9 +367,9 @@
         while not all((c, s) in pumped for s in range(1, hops)):
             pump_next(1)
         def full_sums():
-            sums = dot(w_all[0], c_all[:fsdp_features, place])
+            sums = dot(w_all[0], c_all[c, :fsdp_features])
             for f in range(1, n_fsdp):
-                sums += dot(w_all[f], c_all[f * fsdp_features : (f + 1) * fsdp_features, place])
+                sums += dot(w_all[f], c_all[c, f * fsdp_features : (f + 1) * fsdp_features])
             g_own[:, place] = sums.astype(jnp.bfloat16)
 
         def shard_features(f):
@@ -373,7 +378,7 @@
         if lean:
             @pl.when(is_helper)
             def _():
-                part = dot(w_far[...], c_all[shard_features(far_shard), place])
+                part = dot(w_far[...], c_all[c, shard_features(far_shard)])
                 part_out[:, place] = part.astype(jnp.bfloat16)
                 part_copy(c).start()
                 full_sums()
@@ -381,7 +386,7 @@
             @pl.when(is_end)
             def _():
                 near = 1 - far_shard
-                sums = dot(w_all[near], c_all[shard_features(near), place])
+                sums = dot(w_all[near], c_all[c, shard_features(near)])
                 part_copy(c).wait_recv()
                 g_own[:, place] = (sums + part_in[:, place].astype(jnp.float32)).astype(jnp.bfloat16)
         else:
@@ -494,7 +499,7 @@
         in_specs=[vmem, vmem, vmem, hbm, hbm],
         out_specs=[vmem] * 3,
         scratch_shapes=[
-            pltpu.VMEM((n_tensor * c.shape[0], rows), bf16),
+            pltpu.VMEM((chunks, n_tensor * c.shape[0], CHUNK), bf16),
             pltpu.VMEM((n_fsdp,) + out_weight.shape, bf16),
             pltpu.VMEM((reach,) + k.shape, bf16),
             pltpu.VMEM((reach,) + v.shape, bf16),
@@ -519,7 +524,7 @@
             pltpu.VMEM(out_weight.shape if lean else (16, 128), bf16),
             pltpu.VMEM((out_weight.shape[0], rows) if lean else (16, 128), bf16),
             pltpu.VMEM((out_weight.shape[0], rows) if lean else (16, 128), bf16),
-            dma, dma,
+            dma((chunks,)), dma,
             dma((n_fsdp,)), dma((n_fsdp,)),
             dma((chunks, n_tensor)), dma((chunks, n_tensor)),
             dma((chunks, n_tensor)), dma((chunks, n_tensor)),

time: 65.5 us -> 65.5 us (level)
  no operation moved by 1% of the time
where the time goes in v7:
time: 65.5 us; the launch traced here: 65.4 us
  Pallas kernels  64.7 us (99%)
    pallas_call x1, Pallas kernels, per_device(): pl.pallas_call(functools.partial(kernel, n_seq, n_tensor, n_fsdp, reach),...  62.9 us
    pallas_call x1, Pallas kernels, per_device(): pl.pallas_call(place_kernel, out_shape=[jax.ShapeDtypeStruct(x.shape, bf1...  1.86 us

profile of v7, /device:TPU:0, one launch (start us, length us, event | category | flops | bytes accessed | tf_op | source)
XLA Modules:
  0.0 65.4 jit_solution(10682346448197515837)
XLA Ops:
  0.6 62.9 %shard_map.76 = (bf16[256,512]{1,0:T(8,128)(2,1)}, bf16[256,256]{1,0:T(8,128)(2,1)}, bf16[256,256]{1,0:T(8,128)(2,1)}) custom-call(bf16[256,512]{1,0:T(8,128)(2,1)} %bitcast.10, bf16[256,256]{1,0:T(8,128)(2,1)} %bitcast.12, bf16[256,256]{1,0:T(8,128)(2,1)} %bitcast.13, bf16[1344,256]{1,0:T(8,128)(2,1)} %bitcast.9, bf16[512,2688]{1,0:T(8,128)(2,1)} %w_ref.1), custom_call_target="tpu_custom_call" | custom-call | flops 4000000000 | bytes 8000000 | tf_op jit(solution)/shard_map/pallas_call | solution.py:496
  63.5 1.9 %shard_map.77 = (bf16[256,512]{1,0:T(8,128)(2,1)}, bf16[256,256]{1,0:T(8,128)(2,1)}, bf16[256,256]{1,0:T(8,128)(2,1)}) custom-call(bf16[256,512]{1,0:T(8,128)(2,1)} %get-tuple-element.9.a_in, bf16[256,256]{1,0:T(8,128)(2,1)} %get-tuple-element.10.b_in, bf16[256,256]{1,0:T(8,128)(2,1)} %get-tuple-element.11.c_in), custom_call_target="tpu_custom_call" | custom-call | tf_op jit(solution)/shard_map/pallas_call | solution.py:541
